TPU v7x, 512 devices: a whole 4x4x16 slice. The times are simulated.
512 devices in a mesh: wa: 64 (over x, z), slab: 8 (over y, core).
Axes of the slice: x: 4, y: 4, z: 16, core: 2. Of those that a mesh axis runs over, the one named last changes fastest.
Arguments:
- visibilities: float32 [32768, 2, 128], P(('wa', 'slab')), may hold values from -6 to 6
- row_offset: float32 [32768, 128], P(('wa', 'slab')), may hold values from 0 to 16
- col_offset: float32 [32768, 128], P(('wa', 'slab')), may hold values from 0 to 128
- w_layer: int32 [32768], P(('wa', 'slab')), may hold values from 0 to 63, as said below
- grid_block: int32 [32768], P(('wa', 'slab')), may hold values from 0 to 63
Outputs:
- dirty_image: float32 [512, 1024], P('wa', 'slab')
Inputs may be any that keep to these rules, and one draw needn't show every extreme that they name: `w_layer`: in each device's aligned block of 64 tiles no w-layer is named more than 2 times, and in every draw one w-layer is named exactly 2 times in every block.
All inputs are finite; a program needn't handle non-finite values.
Results may differ from a plain program's by a relative error of at most 0.0003.
Values sent between devices are 32-bit elements; how exact they have to be, the bound alone decides.
No kernel may reach another device: no remote copies, remote signals or barrier semaphores. Data moves between devices by JAX's collectives and lax.ppermute only.
A program may use at most 64 MiB of HBM per device.

v0:
```python
import math

import jax
import jax.numpy as jnp
from jax import lax
from jax.sharding import PartitionSpec as P

NG = 4096
VIS = 128
RB = 16
CB = 128
ROWS_DEV = 32
IMG_L = 512
IMG_M = 1024


kernel_width = 1.0
cell_size = 2.4e-05
w_reach = 20000.0
span_columns = 256


def kernel_rows(offsets, extent):
    centers = jnp.arange(extent, dtype=jnp.float32) + 0.5
    return jnp.exp(-0.5 * ((centers - offsets[..., None]) / kernel_width) ** 2)


def grid_patches(visibilities, row_offset, col_offset):
    row_kernel = kernel_rows(row_offset, RB)
    col_kernel = kernel_rows(col_offset, CB)
    weighted = visibilities[..., :, :, None] * row_kernel[..., None, :, :]
    return jnp.einsum("...xkr,...kc->...xrc", weighted, col_kernel, precision=lax.Precision.HIGHEST)


def screen_phase(w_value, l_index, m_index):
    l_direction = l_index.astype(jnp.float32)[:, None] * cell_size
    m_direction = m_index.astype(jnp.float32)[None, :] * cell_size
    radius = l_direction * l_direction + m_direction * m_direction
    n_lift = -radius / (1.0 + jnp.sqrt(1.0 - radius))
    phase_angle = -2.0 * math.pi * w_value * n_lift
    return (jnp.cos(phase_angle), jnp.sin(phase_angle))


def u_transform(spectrum, u_index, l_index):
    phase_angle = (
        2.0 * math.pi * jnp.mod(l_index[:, None] * u_index[None, :], NG).astype(jnp.float32) / NG
    )
    dft_table = jnp.concatenate([jnp.cos(phase_angle), jnp.sin(phase_angle)], 0)
    product = jnp.dot(dft_table, spectrum, precision=lax.Precision.HIGHEST)
    row_count = l_index.shape[0]
    column_count = spectrum.shape[1] // 2
    cos_part = product[:row_count]
    sin_part = product[row_count:]
    real_part = cos_part[:, :column_count] - sin_part[:, column_count:]
    imag_part = sin_part[:, :column_count] + cos_part[:, column_count:]
    return (real_part, imag_part)


def body(visibilities, row_offset, col_offset, w_layer, grid_block):
    highest = lax.Precision.HIGHEST
    wa_count = lax.axis_size("wa")
    slab_count = lax.axis_size("slab")
    tile_count = w_layer.shape[0]
    capacity = max(2, 2 * tile_count // wa_count)
    slot_count = wa_count * capacity
    layer_hits = (w_layer[:, None] == jnp.arange(wa_count, dtype=jnp.int32)[None, :]).astype(
        jnp.int32
    )
    earlier = jnp.cumsum(layer_hits, axis=0) - layer_hits
    target = w_layer * capacity + jnp.sum(layer_hits * earlier, axis=1)
    placing = jnp.arange(slot_count, dtype=jnp.int32)[:, None] == target[None, :]
    place_float = placing.astype(jnp.float32)
    send_vis = jnp.einsum("st,txk->sxk", place_float, visibilities, precision=highest).reshape(
        wa_count, capacity, 2, VIS
    )
    send_rows = jnp.dot(place_float, row_offset, precision=highest).reshape(wa_count, capacity, VIS)
    send_cols = jnp.dot(place_float, col_offset, precision=highest).reshape(wa_count, capacity, VIS)
    send_block = jnp.dot(placing.astype(jnp.int32), grid_block).reshape(wa_count, capacity)
    vis_piece = lax.all_to_all(send_vis, "wa", split_axis=0, concat_axis=0, tiled=True)
    row_piece = lax.all_to_all(send_rows, "wa", split_axis=0, concat_axis=0, tiled=True)
    col_piece = lax.all_to_all(send_cols, "wa", split_axis=0, concat_axis=0, tiled=True)
    block_piece = lax.all_to_all(send_block, "wa", split_axis=0, concat_axis=0, tiled=True)
    patches = grid_patches(vis_piece, row_piece, col_piece)
    block_total = ROWS_DEV // RB * (NG // CB)
    owner_map = (
        block_piece.reshape(-1)[:, None] == jnp.arange(block_total, dtype=jnp.int32)[None, :]
    ).astype(jnp.float32)
    summed = jnp.einsum(
        "sb,sxrc->bxrc", owner_map, patches.reshape(slot_count, 2, RB, CB), precision=highest
    )
    layer_grid = (
        summed.reshape(ROWS_DEV // RB, NG // CB, 2, RB, CB)
        .transpose(2, 0, 3, 1, 4)
        .reshape(2, ROWS_DEV, NG)
    )
    m_index = jnp.arange(IMG_M, dtype=jnp.int32) - IMG_M // 2
    turn_width = min(span_columns, NG)
    base_angle = (
        2.0
        * math.pi
        * jnp.mod(jnp.arange(turn_width, dtype=jnp.int32)[:, None] * m_index[None, :], NG).astype(
            jnp.float32
        )
        / NG
    )
    cos_base = jnp.cos(base_angle)
    sin_base = jnp.sin(base_angle)
    dft_table = jnp.concatenate(
        [jnp.concatenate([cos_base, sin_base], 1), jnp.concatenate([-sin_base, cos_base], 1)], 0
    )

    def v_turn(turn_index, spectrum):
        start_col = turn_index * turn_width
        left_block = jnp.concatenate(
            [
                lax.dynamic_slice_in_dim(layer_grid[0], start_col, turn_width, 1),
                lax.dynamic_slice_in_dim(layer_grid[1], start_col, turn_width, 1),
            ],
            1,
        )
        product = jnp.dot(left_block, dft_table, precision=highest)
        turn_angle = (
            2.0 * math.pi * jnp.mod((start_col - NG // 2) * m_index, NG).astype(jnp.float32) / NG
        )
        cos_turn = jnp.cos(turn_angle)[None, :]
        sin_turn = jnp.sin(turn_angle)[None, :]
        real_part = product[:, :IMG_M]
        imag_part = product[:, IMG_M:]
        return spectrum + jnp.concatenate(
            [
                real_part * cos_turn - imag_part * sin_turn,
                real_part * sin_turn + imag_part * cos_turn,
            ],
            1,
        )

    spectrum = lax.fori_loop(
        0, NG // turn_width, v_turn, jnp.zeros((ROWS_DEV, 2 * IMG_M), jnp.float32)
    )
    window_rows = ROWS_DEV * slab_count
    l_index = jnp.arange(IMG_L, dtype=jnp.int32) - IMG_L // 2
    layer_number = lax.axis_index("wa").astype(jnp.float32)
    w_value = w_reach * (2.0 * layer_number + 1.0 - wa_count) / wa_count
    spread = 1.0 / (
        2.0 * math.pi * kernel_width**2 * math.sqrt(tile_count * wa_count * slab_count * VIS)
    )
    stacked = spectrum.reshape(ROWS_DEV, 2, IMG_M)
    turned = lax.all_to_all(stacked, "slab", split_axis=2, concat_axis=0, tiled=True)
    column_count = IMG_M // slab_count
    u_index = jnp.arange(window_rows, dtype=jnp.int32) - window_rows // 2
    m_columns = (
        lax.axis_index("slab") * column_count
        + jnp.arange(column_count, dtype=jnp.int32)
        - IMG_M // 2
    )
    real_part, imag_part = u_transform(
        turned.reshape(window_rows, 2 * column_count), u_index, l_index
    )
    cos_screen, sin_screen = screen_phase(w_value, l_index, m_columns)
    layer_image = (real_part * cos_screen - imag_part * sin_screen) * spread
    image_total = lax.psum(layer_image, "wa")
    own_rows = IMG_L // wa_count
    return lax.dynamic_slice_in_dim(image_total, lax.axis_index("wa") * own_rows, own_rows, 0)


def solution(mesh):
    placed = (
        P(("wa", "slab"), None, None),
        P(("wa", "slab"), None),
        P(("wa", "slab"), None),
        P(("wa", "slab")),
        P(("wa", "slab")),
    )
    return jax.shard_map(
        body, mesh=mesh, in_specs=placed, out_specs=P("wa", "slab"), check_vma=False
    )
```

profile of v0, /device:TPU:24, one launch (start us, length us, event | category | flops | bytes accessed | tf_op | source)
XLA Modules:
  0.0 473.1 jit_solution(16766662186786091645)
XLA Ops:
  10.5 18.6 %all-to-all-start = ((s32[64,1,2]{2,1,0:T(1,128)}), s32[64,1,2]{2,1,0:T(1,128)S(1)}, u32[]{:S(2)}, u32[]{:S(2)}) async-start(s32[64,1,2]{2,1,0:T(1,128)} %bitcast.2), calls=%async_computation | async-start | bytes 65536 | tf_op jit(solution)/shard_map/all_to_all | solution.py:82
  31.9 11.5 %all-to-all-done = s32[64,1,2]{2,1,0:T(1,128)S(1)} async-done(((s32[64,1,2]{2,1,0:T(1,128)}), s32[64,1,2]{2,1,0:T(1,128)S(1)}, u32[]{:S(2)}, u32[]{:S(2)}) %all-to-all-start) | async-done | bytes 544 | tf_op jit(solution)/shard_map/all_to_all | solution.py:82
  52.1 10.6 %all-to-all-done.2 = f32[64,2,128]{2,1,0:T(2,128)S(1)} async-done(((f32[64,2,128]{2,1,0:T(2,128)}), f32[64,2,128]{2,1,0:T(2,128)S(1)}, u32[]{:S(2)}, u32[]{:S(2)}) %all-to-all-start.2) | async-done | bytes 65568 | tf_op jit(solution)/shard_map/all_to_all | solution.py:80
  70.4 12.1 %all-to-all-done.1 = f32[64,2,2,128]{3,1,2,0:T(2,128)S(1)} async-done(((f32[64,2,2,128]{3,1,2,0:T(2,128)}), f32[64,2,2,128]{3,1,2,0:T(2,128)S(1)}, u32[]{:S(2)}, u32[]{:S(2)}) %all-to-all-start.1) | async-done | bytes 131104 | tf_op jit(solution)/shard_map/all_to_all | solution.py:79
  82.4 5.6 %all-to-all-start.3 = ((f32[64,2,128]{2,1,0:T(2,128)}), f32[64,2,128]{2,1,0:T(2,128)S(1)}, u32[]{:S(2)}, u32[]{:S(2)}) async-start(f32[64,2,128]{2,1,0:T(2,128)} %bitcast.8), calls=%async_computation.3 | async-start | bytes 131072 | tf_op jit(solution)/shard_map/all_to_all | solution.py:81
  89.8 12.7 %all-to-all-done.3 = f32[64,2,128]{2,1,0:T(2,128)S(1)} async-done(((f32[64,2,128]{2,1,0:T(2,128)}), f32[64,2,128]{2,1,0:T(2,128)S(1)}, u32[]{:S(2)}, u32[]{:S(2)}) %all-to-all-start.3) | async-done | bytes 65568 | tf_op jit(solution)/shard_map/all_to_all | solution.py:81
  102.5 8.4 %fusion.12 = f32[64,2,2,16,128]{4,3,2,1,0:T(8,128)S(1)} fusion(f32[64,2,128]{2,1,0:T(2,128)S(1)} %all-to-all-done.3, f32[128]{0:T(128)S(1)} %iota_add_fusion.3, f32[64,2,128,16]{2,3,1,0:T(8,128)S(1)} %multiply_exponential_fusion, f32[64,2,2,128]{3,2,1,0:T(2,128)S(1)} %copy.30), kind=kOutput, calls=%fused_computation.20 | convolution fusion | flops 812122112 | bytes 3342848 | tf_op jit(solution)/shard_map/...xkr,...kc->...xrc/dot_general | solution.py:32
  113.2 80.0 %while.16 = (s32[]{:T(128)}, f32[32,2048]{1,0:T(8,128)S(1)}, f32[2,32,4096]{2,1,0:T(8,128)S(1)}, f32[512,2048]{1,0:T(8,128)}, s32[]{:T(128)}, /*index=5*/s32[]{:T(128)}, s32[]{:T(128)}, s32[]{:T(128)}, s32[]{:T(128)}) while((s32[]{:T(128)}, f32[32,2048]{1,0:T(8,128)S(1)}, f32[2,32,4096]{2,1,0:T(8,128)S(1)}, f32[512,2048]{1,0:T(8,128)}, ...), condition=%wide.region_3.4_spmd.clone, body=%wide.region_2.3_spmd.clone.sunk | while | flops 403078144 | bytes 8077481 | solution.py:137
  113.5 4.7 fusion.88
  118.5 4.7 fusion.88
  123.5 4.7 fusion.88
  128.5 4.7 fusion.88
  133.5 4.7 fusion.88
  138.5 4.7 fusion.88
  143.5 4.7 fusion.88
  148.4 4.7 fusion.88
  153.4 4.7 fusion.88
  158.4 4.7 fusion.88
  163.4 4.7 fusion.88
  173.4 4.7 fusion.88
  178.4 4.7 fusion.88
  183.3 4.7 fusion.88
  195.7 4.7 all-to-all-start.4
  212.1 252.9 %all-reduce.2.cloned.1.call-done = f32[512,128]{1,0:T(8,128)} async-done(((f32[512,128]{1,0:T(8,128)}), f32[512,128]{1,0:T(8,128)}) %all-reduce.2.cloned.1.call-update) | async-done | bytes 262160 | tf_op jit(solution)/shard_map/psum | solution.py:161
  (132 shorter events, 56.0 us)
Async XLA Ops:
  6.5 24.3 %copy-start = (f32[64,2,128]{2,1,0:T(2,128)S(1)}, f32[64,2,128]{2,1,0:T(2,128)}, u32[]{:S(2)}) copy-start(f32[64,2,128]{2,1,0:T(2,128)} %param.7) | copy-start | bytes 196612
  6.5 60.7 %copy-start.1 = (f32[64,128]{1,0:T(8,128)S(1)}, f32[64,128]{1,0:T(8,128)}, u32[]{:S(2)}) copy-start(f32[64,128]{1,0:T(8,128)} %param.9) | copy-start | bytes 98308
  10.5 32.8 %all-to-all-start = ((s32[64,1,2]{2,1,0:T(1,128)}), s32[64,1,2]{2,1,0:T(1,128)S(1)}, u32[]{:S(2)}, u32[]{:S(2)}) async-start(s32[64,1,2]{2,1,0:T(1,128)} %bitcast.2), calls=%async_computation | async-start | bytes 65536 | tf_op jit(solution)/shard_map/all_to_all | solution.py:82
  43.3 19.3 %all-to-all-start.2 = ((f32[64,2,128]{2,1,0:T(2,128)}), f32[64,2,128]{2,1,0:T(2,128)S(1)}, u32[]{:S(2)}, u32[]{:S(2)}) async-start(f32[64,2,128]{2,1,0:T(2,128)} %bitcast.7), calls=%async_computation.2 | async-start | bytes 131072 | tf_op jit(solution)/shard_map/all_to_all | solution.py:80
  62.6 19.8 %all-to-all-start.1 = ((f32[64,2,2,128]{3,1,2,0:T(2,128)}), f32[64,2,2,128]{3,1,2,0:T(2,128)S(1)}, u32[]{:S(2)}, u32[]{:S(2)}) async-start(f32[64,2,2,128]{3,1,2,0:T(2,128)} %copy.29), calls=%async_computation.1 | async-start | bytes 262144 | tf_op jit(solution)/shard_map/all_to_all | solution.py:79
  82.4 20.0 %all-to-all-start.3 = ((f32[64,2,128]{2,1,0:T(2,128)}), f32[64,2,128]{2,1,0:T(2,128)S(1)}, u32[]{:S(2)}, u32[]{:S(2)}) async-start(f32[64,2,128]{2,1,0:T(2,128)} %bitcast.8), calls=%async_computation.3 | async-start | bytes 131072 | tf_op jit(solution)/shard_map/all_to_all | solution.py:81
  195.7 10.2 %all-to-all-start.4 = ((f32[8,1,8192]{2,1,0:T(1,128)}), f32[8,1,8192]{2,1,0:T(1,128)S(1)}, u32[]{:S(2)}, u32[]{:S(2)}) async-start(f32[8,1,8192]{2,1,0:T(1,128)} %reshape.148), calls=%async_computation.4 | async-start | bytes 524288 | tf_op jit(solution)/shard_map/all_to_all | solution.py:148
  200.4 264.6 %all-reduce.2.cloned.1.call-start = ((), (), s32[]{:S(2)}) async-start(), calls=%async_computation.5 | async-start | bytes 524288 | tf_op jit(solution)/shard_map/psum | solution.py:161
Sparse Core Ops, SparseCore 0:
  212.2 252.7 all-reduce.1
where the time goes:
time: 474 us; the launch traced here: 473 us
  waiting for transfers between devices  303 us (64%)
  matrix products  89.9 us (19%)
  starting transfers between devices  38 us (8%)
  other arithmetic  17.7 us (4%)
  between operations  13.6 us (3%)
  local copies, waits for them, and re-layouts  9.53 us (2%)
    psum x1, waiting for transfers between devices, body(): image_total = lax.psum(layer_image, 'wa')  253 us
    dot_general x16, matrix products, v_turn(): product = jnp.dot(left_block, dft_table, precision=highest)  74.6 us
    all_to_all x1, starting transfers between devices, body(): lax.all_to_all(send_block, 'wa', split_axis=0, concat_axis=0, tiled=True)  18.6 us
    all_to_all x1, waiting for transfers between devices, body(): lax.all_to_all(send_cols, 'wa', split_axis=0, concat_axis=0, tiled=True)  12.7 us
    all_to_all x1, waiting for transfers between devices, body(): lax.all_to_all(send_vis, 'wa', split_axis=0, concat_axis=0, tiled=True)  12.1 us
    all_to_all x1, waiting for transfers between devices, body(): lax.all_to_all(send_block, 'wa', split_axis=0, concat_axis=0, tiled=True)  11.5 us
    all_to_all x1, waiting for transfers between devices, body(): lax.all_to_all(send_rows, 'wa', split_axis=0, concat_axis=0, tiled=True)  10.6 us
  transfers between devices with their start and end apart: 6, of which 6 were waited for; matrix products, arithmetic and copies ran while one was open for 3% of the time, Pallas kernels for 0%

commit v1 on v0

v1 whole, which is shorter than its diff:
```python
import math

import numpy as np

import jax
import jax.numpy as jnp
from jax import lax
from jax.sharding import PartitionSpec as P

NG = 4096
VIS = 128
RB = 16
CB = 128
ROWS_DEV = 32
IMG_L = 512
IMG_M = 1024
CAP = 2
X_CHIPS = 4
SUB = 32


kernel_width = 1.0
cell_size = 2.4e-05
w_reach = 20000.0


def kernel_rows(offsets, extent):
    centers = jnp.arange(extent, dtype=jnp.float32) + 0.5
    return jnp.exp(-0.5 * ((centers - offsets[..., None]) / kernel_width) ** 2)


def screen_phase(w_value, l_index, m_index):
    l_direction = l_index.astype(jnp.float32)[:, None] * cell_size
    m_direction = m_index.astype(jnp.float32)[None, :] * cell_size
    radius = l_direction * l_direction + m_direction * m_direction
    n_lift = -radius / (1.0 + jnp.sqrt(1.0 - radius))
    phase_angle = -2.0 * math.pi * w_value * n_lift
    return (jnp.cos(phase_angle), jnp.sin(phase_angle))


def wave(turns, period):
    angle = 2.0 * np.pi * (np.asarray(turns) % period) / period
    return np.cos(angle), np.sin(angle)


def real_form(cos_part, sin_part):
    return np.stack([np.stack([cos_part, sin_part]), np.stack([-sin_part, cos_part])]).astype(
        np.float32
    )


def body(visibilities, row_offset, col_offset, w_layer, grid_block):
    highest = lax.Precision.HIGHEST
    high = lax.Precision.HIGH
    wa_count = lax.axis_size("wa")
    slab_count = lax.axis_size("slab")
    tile_count = w_layer.shape[0]
    slot_count = wa_count * CAP
    layer_hits = (w_layer[:, None] == w_layer[None, :]) & (
        jnp.arange(tile_count)[:, None] > jnp.arange(tile_count)[None, :]
    )
    target = w_layer * CAP + jnp.sum(layer_hits.astype(jnp.int32), axis=1)
    placing = (jnp.arange(slot_count, dtype=jnp.int32)[:, None] == target[None, :]).astype(
        jnp.float32
    )
    z_count = wa_count // X_CHIPS
    own_x = lax.axis_index("wa") // z_count
    z_groups = [[x * z_count + z for z in range(z_count)] for x in range(X_CHIPS)]

    def to_x(step):
        return [
            (x * z_count + z, (x + step) % X_CHIPS * z_count + z)
            for x in range(X_CHIPS)
            for z in range(z_count)
        ]

    tile_row = jnp.concatenate(
        [
            visibilities.reshape(tile_count, 2 * VIS),
            row_offset,
            col_offset,
            jnp.broadcast_to(grid_block.astype(jnp.float32)[:, None], (tile_count, 64)),
        ],
        1,
    )
    width = tile_row.shape[1]
    sent = jnp.dot(placing, tile_row, precision=highest).reshape(X_CHIPS, z_count, CAP * width)
    sent = jnp.swapaxes(sent, 0, 1).reshape(z_count, 1, X_CHIPS * CAP * width)
    got = lax.all_to_all(
        sent, "wa", split_axis=0, concat_axis=0, tiled=True, axis_index_groups=z_groups
    )
    got = got.reshape(z_count, X_CHIPS, CAP * width).swapaxes(0, 1)
    chunks = [
        lax.dynamic_index_in_dim(got, (own_x + step) % X_CHIPS, 0, False) for step in range(X_CHIPS)
    ]
    got = jnp.stack(
        chunks[:1] + [lax.ppermute(chunks[step], "wa", to_x(step)) for step in range(1, X_CHIPS)]
    )
    got = got.reshape(slot_count, width)
    vis_piece = got[:, : 2 * VIS].reshape(slot_count, 2, VIS)
    row_piece = got[:, 2 * VIS : 3 * VIS]
    col_piece = got[:, 3 * VIS : 4 * VIS]
    block_piece = got[:, 4 * VIS].astype(jnp.int32)

    weighted = vis_piece[:, :, None, :] * jnp.swapaxes(kernel_rows(row_piece, RB), 1, 2)[:, None]
    patches = jnp.einsum("txrk,tkc->txrc", weighted, kernel_rows(col_piece, CB), precision=high)

    q = np.arange(SUB)
    turn = jnp.asarray(
        (real_form(*wave(q[:, None] * q[None, :], SUB)) * (1 - 2 * (q % 2))).astype(np.float32)
    )
    half = ROWS_DEV // RB
    block_hot = (block_piece[:, None] == jnp.arange(half * SUB)[None, :]).astype(jnp.float32)
    turns = jnp.einsum(
        "thb,xybq->txhyq", block_hot.reshape(slot_count, half, SUB), turn, precision=highest
    )
    along_b = jnp.einsum("txhyq,txrc->hryqc", turns, patches, precision=high)
    c = np.arange(CB)
    cos_twist, sin_twist = (
        jnp.asarray(part.astype(np.float32)) for part in wave(q[:, None] * c[None, :], NG)
    )
    real_b, imag_b = along_b[:, :, 0], along_b[:, :, 1]
    twisted = jnp.stack(
        [real_b * cos_twist - imag_b * sin_twist, real_b * sin_twist + imag_b * cos_twist], 2
    )
    last = jnp.asarray(real_form(*wave(c[:, None] * (q[None, :] - SUB // 2), CB)))
    spectrum = jnp.einsum("hryqc,yzcn->hrznq", twisted, last, precision=high)
    columns = IMG_M // slab_count
    pieces = spectrum.reshape(ROWS_DEV, 2, slab_count, columns).transpose(2, 0, 1, 3)
    pieces = pieces.reshape(slab_count, 2 * ROWS_DEV, columns)
    turned = lax.all_to_all(pieces, "slab", split_axis=0, concat_axis=0, tiled=True)

    window_rows = ROWS_DEV * slab_count
    rows = np.arange(window_rows) - window_rows // 2
    lines = np.arange(IMG_L) - IMG_L // 2
    spread = 1.0 / (
        2.0 * math.pi * kernel_width**2 * math.sqrt(tile_count * wa_count * slab_count * VIS)
    )
    u_table = jnp.asarray(
        real_form(*wave(lines[:, None] * rows[None, :], NG)).transpose(1, 2, 3, 0).reshape(
            2 * IMG_L, 2 * window_rows
        )
        * np.float32(spread)
    )
    image = jnp.dot(u_table, turned.reshape(2 * window_rows, columns), precision=high)
    l_index = jnp.arange(IMG_L, dtype=jnp.int32) - IMG_L // 2
    m_index = lax.axis_index("slab") * columns + jnp.arange(columns, dtype=jnp.int32) - IMG_M // 2
    layer_number = lax.axis_index("wa").astype(jnp.float32)
    w_value = w_reach * (2.0 * layer_number + 1.0 - wa_count) / wa_count
    cos_screen, sin_screen = screen_phase(w_value, l_index, m_index)
    layer_image = image[:IMG_L] * cos_screen - image[IMG_L:] * sin_screen
    layer_image = layer_image.reshape(X_CHIPS, IMG_L // X_CHIPS, columns)
    parts = [
        lax.dynamic_index_in_dim(layer_image, (own_x + step) % X_CHIPS, 0, False)
        for step in range(X_CHIPS)
    ]
    part_sum = parts[0]
    for step in range(1, X_CHIPS):
        part_sum = part_sum + lax.ppermute(parts[step], "wa", to_x(step))
    shares = lax.all_to_all(
        part_sum.reshape(z_count, IMG_L // wa_count, columns),
        "wa",
        split_axis=0,
        concat_axis=0,
        tiled=True,
        axis_index_groups=z_groups,
    )
    return jnp.sum(shares, 0)


def solution(mesh):
    placed = (
        P(("wa", "slab"), None, None),
        P(("wa", "slab"), None),
        P(("wa", "slab"), None),
        P(("wa", "slab")),
        P(("wa", "slab")),
    )
    return jax.shard_map(
        body, mesh=mesh, in_specs=placed, out_specs=P("wa", "slab"), check_vma=False
    )
```

time: 474 us -> 113 us (0.24)
  the two profiles are of different devices: /device:TPU:24 before, /device:TPU:32 now
where the time goes in v1:
time: 113 us; the launch traced here: 112 us
  starting transfers between devices  38.5 us (34%)
  waiting for transfers between devices  35.1 us (31%)
  blocking collectives  18.4 us (16%)
  matrix products  9.39 us (8%)
  other arithmetic  5.4 us (5%)
  local copies, waits for them, and re-layouts  4.87 us (4%)
    all_to_all x1, waiting for transfers between devices, body(): lax.all_to_all(sent, 'wa', split_axis=0, concat_axis=0, tiled=True, axis_...  18.7 us
    all_to_all x1, blocking collectives, body(): lax.all_to_all(part_sum.reshape(z_count, IMG_L // wa_count, columns), 'wa...  18.4 us
    all_to_all x1, starting transfers between devices, body(): lax.all_to_all(sent, 'wa', split_axis=0, concat_axis=0, tiled=True, axis_...  15.2 us
    ppermute x3, starting transfers between devices, body(): lax.ppermute(chunks[step], 'wa', to_x(step))  10.2 us
    ppermute x3, starting transfers between devices, body(): part_sum = part_sum + lax.ppermute(parts[step], 'wa', to_x(step))  8.66 us
    all_to_all x1, waiting for transfers between devices, body(): lax.all_to_all(pieces, 'slab', split_axis=0, concat_axis=0, tiled=True)  7.52 us
    dot_general x1, matrix products, body(): jnp.einsum('txrk,tkc->txrc', weighted, kernel_rows(col_piece, CB), precis...  4.65 us
    ppermute x3, waiting for transfers between devices, body(): lax.ppermute(chunks[step], 'wa', to_x(step))  4.62 us
  transfers between devices with their start and end apart: 8, of which 6 were waited for; matrix products, arithmetic and copies ran while one was open for 0% of the time, Pallas kernels for 0%

profile of v1, /device:TPU:32, one launch (start us, length us, event | category | flops | bytes accessed | tf_op | source)
XLA Modules:
  0.0 112.1 jit_solution(10055500865433556196)
XLA Ops:
  0.7 0.8 copy.72
  1.5 0.9 convert_reduce_fusion
  3.2 1.1 fusion.28
  4.5 1.1 reshape.111
  5.5 15.2 %all-to-all-start = ((f32[16,1,4608]{2,1,0:T(1,128)}), f32[16,1,4608]{2,1,0:T(1,128)S(1)}, u32[]{:S(2)}, u32[]{:S(2)}) async-start(f32[16,1,4608]{2,1,0:T(1,128)} %reshape.111), calls=%async_computation | async-start | bytes 589824 | tf_op jit(solution)/shard_map/all_to_all | solution.py:89
  20.7 18.7 %all-to-all-done = f32[16,1,4608]{2,1,0:T(1,128)S(1)} async-done(((f32[16,1,4608]{2,1,0:T(1,128)}), f32[16,1,4608]{2,1,0:T(1,128)S(1)}, u32[]{:S(2)}, u32[]{:S(2)}) %all-to-all-start) | async-done | bytes 294944 | tf_op jit(solution)/shard_map/all_to_all | solution.py:89
  40.6 4.7 %collective-permute-start.2 = (f32[16,1152]{1,0:T(8,128)S(1)}, f32[16,1152]{1,0:T(8,128)S(1)}, u32[]{:S(2)}, u32[]{:S(2)}) collective-permute-start(f32[16,1152]{1,0:T(8,128)S(1)} %bitcast.94), channel_id=1, source_target_pairs={{0,384},{8,392},{16,400},{24,408},{32,416},{40,424},{48,432},{56,4... | collective-permute-start | bytes 221192 | tf_op jit(solution)/shard_map/ppermute | solution.py:97
  45.3 2.7 %collective-permute-start.1 = (f32[16,1152]{1,0:T(8,128)S(1)}, f32[16,1152]{1,0:T(8,128)S(1)}, u32[]{:S(2)}, u32[]{:S(2)}) collective-permute-start(f32[16,1152]{1,0:T(8,128)S(1)} %bitcast.95), channel_id=1, source_target_pairs={{0,256},{8,264},{16,272},{24,280},{32,288},{40,296},{48,304},{56,3... | collective-permute-start | bytes 221192 | tf_op jit(solution)/shard_map/ppermute | solution.py:97
  48.0 2.8 %collective-permute-start = (f32[16,1152]{1,0:T(8,128)S(1)}, f32[16,1152]{1,0:T(8,128)S(1)}, u32[]{:S(2)}, u32[]{:S(2)}) collective-permute-start(f32[16,1152]{1,0:T(8,128)S(1)} %bitcast.96), channel_id=1, source_target_pairs={{0,128},{8,136},{16,144},{24,152},{32,160},{40,168},{48,176},{56,1... | collective-permute-start | bytes 221192 | tf_op jit(solution)/shard_map/ppermute | solution.py:97
  50.9 3.0 %collective-permute-done.1 = f32[16,1152]{1,0:T(8,128)S(1)} collective-permute-done((f32[16,1152]{1,0:T(8,128)S(1)}, f32[16,1152]{1,0:T(8,128)S(1)}, u32[]{:S(2)}, u32[]{:S(2)}) %collective-permute-start.1) | collective-permute-done | bytes 73760 | tf_op jit(solution)/shard_map/ppermute | solution.py:97
  53.8 1.6 %collective-permute-done = f32[16,1152]{1,0:T(8,128)S(1)} collective-permute-done((f32[16,1152]{1,0:T(8,128)S(1)}, f32[16,1152]{1,0:T(8,128)S(1)}, u32[]{:S(2)}, u32[]{:S(2)}) %collective-permute-start) | collective-permute-done | bytes 73760 | tf_op jit(solution)/shard_map/ppermute | solution.py:97
  56.4 4.7 %fusion.12 = f32[128,2,16,128,1,1]{3,2,1,0,5,4:T(8,128)S(1)} fusion(f32[128,128]{1,0:T(8,128)S(1)} %get-tuple-element.8, f32[128]{0:T(128)S(1)} %iota_add_fusion, f32[128,16,128]{2,1,0:T(8,128)S(1)} %multiply_exponential_fusion, f32[128,2,128]{2,1,0:T(2,128)S(1)} %mul.125), kind=kOutput, calls=%fused_computation.12 | convolution fusion | flops 409468928 | bytes 3342848 | tf_op jit(solution)/shard_map/txrk,tkc->txrc/dot_general | solution.py:106
  61.0 1.8 %fusion.17 = f32[2,16,2,32,128]{4,3,2,0,1:T(8,128)S(1)} fusion(f32[128,2,2,2,32,1]{0,4,1,3,2,5:T(8,128)S(1)} %convolution_bitcast_fusion.1, f32[128,2,16,128,1,1]{3,2,1,0,5,4:T(8,128)S(1)} %fusion.12), kind=kOutput, calls=%fused_computation.13 | convolution fusion | flops 402653184 | bytes 3276800 | tf_op jit(solution)/shard_map/txhyq,txrc->hryqc/dot_general | solution.py:117
  65.0 0.7 copy.39
  65.7 4.5 %all-to-all-start.1 = ((f32[8,64,128]{2,1,0:T(8,128)}), f32[8,64,128]{2,1,0:T(8,128)S(1)}, u32[]{:S(2)}, u32[]{:S(2)}) async-start(f32[8,64,128]{2,1,0:T(8,128)} %copy.39), calls=%async_computation.1 | async-start | bytes 524288 | tf_op jit(solution)/shard_map/all_to_all | solution.py:131
  70.2 7.5 %all-to-all-done.1 = f32[8,64,128]{2,1,0:T(8,128)S(1)} async-done(((f32[8,64,128]{2,1,0:T(8,128)}), f32[8,64,128]{2,1,0:T(8,128)S(1)}, u32[]{:S(2)}, u32[]{:S(2)}) %all-to-all-start.1) | async-done | bytes 262176 | tf_op jit(solution)/shard_map/all_to_all | solution.py:131
  77.8 1.0 fusion.49
  78.8 1.3 %fusion.27 = f32[512,128]{1,0:T(8,128)S(1)} fusion(f32[1024,128]{1,0:T(8,128)S(1)} %fusion.49, f32[128]{0:T(128)S(1)} %multiply_multiply_fusion.1, f32[512]{0:T(512)S(1)} %multiply_multiply_fusion, f32[]{:T(128)S(6)} %mul_shard_map.8), kind=kLoop, calls=%fused_computation.31 | loop fusion | flops 589824 | bytes 788996 | tf_op jit(solution)/shard_map/sub | solution.py:151
  80.1 2.0 %collective-permute-start.5 = (f32[128,128]{1,0:T(8,128)S(1)}, f32[128,128]{1,0:T(8,128)S(1)}, u32[]{:S(2)}, u32[]{:S(2)}) collective-permute-start(f32[128,128]{1,0:T(8,128)S(1)} %get-tuple-element.14), channel_id=1, source_target_pairs={{0,384},{8,392},{16,400},{24,408},{32,416},{40,424},{48,432},{56,4... | collective-permute-start | bytes 196616 | tf_op jit(solution)/shard_map/ppermute | solution.py:159
  82.1 3.6 %collective-permute-start.4 = (f32[128,128]{1,0:T(8,128)S(1)}, f32[128,128]{1,0:T(8,128)S(1)}, u32[]{:S(2)}, u32[]{:S(2)}) collective-permute-start(f32[128,128]{1,0:T(8,128)S(1)} %get-tuple-element.15), channel_id=1, source_target_pairs={{0,256},{8,264},{16,272},{24,280},{32,288},{40,296},{48,304},{56,3... | collective-permute-start | bytes 196616 | tf_op jit(solution)/shard_map/ppermute | solution.py:159
  85.6 3.1 %collective-permute-start.3 = (f32[128,128]{1,0:T(8,128)S(1)}, f32[128,128]{1,0:T(8,128)S(1)}, u32[]{:S(2)}, u32[]{:S(2)}) collective-permute-start(f32[128,128]{1,0:T(8,128)S(1)} %get-tuple-element.13), channel_id=1, source_target_pairs={{0,128},{8,136},{16,144},{24,152},{32,160},{40,168},{48,176},{56,1... | collective-permute-start | bytes 196616 | tf_op jit(solution)/shard_map/ppermute | solution.py:159
  88.8 1.0 collective-permute-done.4
  89.7 3.3 %collective-permute-done.3 = f32[128,128]{1,0:T(8,128)S(1)} collective-permute-done((f32[128,128]{1,0:T(8,128)S(1)}, f32[128,128]{1,0:T(8,128)S(1)}, u32[]{:S(2)}, u32[]{:S(2)}) %collective-permute-start.3) | collective-permute-done | bytes 65568 | tf_op jit(solution)/shard_map/ppermute | solution.py:159
  93.0 18.4 %all_to_all.15 = f32[16,8,128]{2,1,0:T(8,128)S(1)} all-to-all(f32[16,8,128]{2,1,0:T(8,128)S(1)} %fusion.39), channel_id=1, replica_groups={{0,8,16,24,32,40,48,56,64,72,80,88,96,104,112,120},{128,136,144,152,160..., dimensions={0} | all-to-all | bytes 131072 | tf_op jit(solution)/shard_map/all_to_all | solution.py:160
  (44 shorter events, 6.3 us)
Async XLA Ops:
  5.5 34.0 %all-to-all-start = ((f32[16,1,4608]{2,1,0:T(1,128)}), f32[16,1,4608]{2,1,0:T(1,128)S(1)}, u32[]{:S(2)}, u32[]{:S(2)}) async-start(f32[16,1,4608]{2,1,0:T(1,128)} %reshape.111), calls=%async_computation | async-start | bytes 589824 | tf_op jit(solution)/shard_map/all_to_all | solution.py:89
  40.3 15.8 %copy-start.2 = (f32[2,2,32,32,1]{2,3,0,1,4:T(8,128)S(1)}, f32[2,2,32,32,1]{2,3,0,1,4:T(8,128)}, u32[]{:S(2)}) copy-start(f32[2,2,32,32,1]{2,3,0,1,4:T(8,128)} %constant.140) | copy-start | bytes 49156
  40.6 10.3 %collective-permute-start.2 = (f32[16,1152]{1,0:T(8,128)S(1)}, f32[16,1152]{1,0:T(8,128)S(1)}, u32[]{:S(2)}, u32[]{:S(2)}) collective-permute-start(f32[16,1152]{1,0:T(8,128)S(1)} %bitcast.94), channel_id=1, source_target_pairs={{0,384},{8,392},{16,400},{24,408},{32,416},{40,424},{48,432},{56,4... | collective-permute-start | bytes 221192 | tf_op jit(solution)/shard_map/ppermute | solution.py:97
  45.3 8.5 %collective-permute-start.1 = (f32[16,1152]{1,0:T(8,128)S(1)}, f32[16,1152]{1,0:T(8,128)S(1)}, u32[]{:S(2)}, u32[]{:S(2)}) collective-permute-start(f32[16,1152]{1,0:T(8,128)S(1)} %bitcast.95), channel_id=1, source_target_pairs={{0,256},{8,264},{16,272},{24,280},{32,288},{40,296},{48,304},{56,3... | collective-permute-start | bytes 221192 | tf_op jit(solution)/shard_map/ppermute | solution.py:97
  48.0 7.5 %collective-permute-start = (f32[16,1152]{1,0:T(8,128)S(1)}, f32[16,1152]{1,0:T(8,128)S(1)}, u32[]{:S(2)}, u32[]{:S(2)}) collective-permute-start(f32[16,1152]{1,0:T(8,128)S(1)} %bitcast.96), channel_id=1, source_target_pairs={{0,128},{8,136},{16,144},{24,152},{32,160},{40,168},{48,176},{56,1... | collective-permute-start | bytes 221192 | tf_op jit(solution)/shard_map/ppermute | solution.py:97
  61.0 1.9 %copy-start.3 = (f32[32,128]{1,0:T(8,128)S(1)}, f32[32,128]{1,0:T(8,128)}, u32[]{:S(2)}) copy-start(f32[32,128]{1,0:T(8,128)} %constant.132.clone) | copy-start | bytes 49156
  61.0 1.9 %copy-start.4 = (f32[32,128]{1,0:T(8,128)S(1)}, f32[32,128]{1,0:T(8,128)}, u32[]{:S(2)}) copy-start(f32[32,128]{1,0:T(8,128)} %constant.131.clone) | copy-start | bytes 49156
  62.9 0.8 copy-start.1
  64.7 13.1 %copy-start = (f32[1024,512]{1,0:T(8,128)S(1)}, f32[1024,512]{1,0:T(8,128)}, u32[]{:S(2)}) copy-start(f32[1024,512]{1,0:T(8,128)} %constant.134.clone) | copy-start | bytes 6291460
  65.7 12.0 %all-to-all-start.1 = ((f32[8,64,128]{2,1,0:T(8,128)}), f32[8,64,128]{2,1,0:T(8,128)S(1)}, u32[]{:S(2)}, u32[]{:S(2)}) async-start(f32[8,64,128]{2,1,0:T(8,128)} %copy.39), calls=%async_computation.1 | async-start | bytes 524288 | tf_op jit(solution)/shard_map/all_to_all | solution.py:131
  80.1 8.7 %collective-permute-start.5 = (f32[128,128]{1,0:T(8,128)S(1)}, f32[128,128]{1,0:T(8,128)S(1)}, u32[]{:S(2)}, u32[]{:S(2)}) collective-permute-start(f32[128,128]{1,0:T(8,128)S(1)} %get-tuple-element.14), channel_id=1, source_target_pairs={{0,384},{8,392},{16,400},{24,408},{32,416},{40,424},{48,432},{56,4... | collective-permute-start | bytes 196616 | tf_op jit(solution)/shard_map/ppermute | solution.py:159
  82.1 7.7 %collective-permute-start.4 = (f32[128,128]{1,0:T(8,128)S(1)}, f32[128,128]{1,0:T(8,128)S(1)}, u32[]{:S(2)}, u32[]{:S(2)}) collective-permute-start(f32[128,128]{1,0:T(8,128)S(1)} %get-tuple-element.15), channel_id=1, source_target_pairs={{0,256},{8,264},{16,272},{24,280},{32,288},{40,296},{48,304},{56,3... | collective-permute-start | bytes 196616 | tf_op jit(solution)/shard_map/ppermute | solution.py:159
  85.6 7.4 %collective-permute-start.3 = (f32[128,128]{1,0:T(8,128)S(1)}, f32[128,128]{1,0:T(8,128)S(1)}, u32[]{:S(2)}, u32[]{:S(2)}) collective-permute-start(f32[128,128]{1,0:T(8,128)S(1)} %get-tuple-element.13), channel_id=1, source_target_pairs={{0,128},{8,136},{16,144},{24,152},{32,160},{40,168},{48,176},{56,1... | collective-permute-start | bytes 196616 | tf_op jit(solution)/shard_map/ppermute | solution.py:159

commit v2 on v1

v2 whole, which is shorter than its diff:
```python
import math

import ml_dtypes
import numpy as np

import jax
import jax.numpy as jnp
from jax import lax
from jax.experimental import pallas as pl
from jax.experimental.pallas import tpu as pltpu
from jax.sharding import Mesh
from jax.sharding import PartitionSpec as P

NG = 4096
VIS = 128
RB = 16
CB = 128
ROWS_DEV = 32
IMG_L = 512
IMG_M = 1024
CAP = 2
LAYERS = 64
N_SLAB = 8
X_CHIPS = 4
Z_CHIPS = 16
SUB = 32
SLOTS = LAYERS * CAP
LANES = 128
SENT = 4 * CAP + 1
PEERS = X_CHIPS * N_SLAB
PAIRS = RB // 2


kernel_width = 1.0
cell_size = 2.4e-05
w_reach = 20000.0

f32 = jnp.float32
bf16 = jnp.bfloat16
VMEM = pl.BlockSpec(memory_space=pltpu.VMEM)
SMEM = pl.BlockSpec(memory_space=pltpu.SMEM)
NT = (((1,), (1,)), ((), ()))
NN = (((1,), (0,)), ((), ()))


def wave(turns, period):
    angle = 2.0 * np.pi * (np.asarray(turns) % period) / period
    return np.cos(angle), np.sin(angle)


def np_split(table):
    table = np.asarray(table, np.float32)
    upper = table.astype(ml_dtypes.bfloat16)
    return upper, (table - upper.astype(np.float32)).astype(ml_dtypes.bfloat16)


def split(value):
    upper = value.astype(bf16)
    return upper, (value - upper.astype(f32)).astype(bf16)


def dot(left, right, dims):
    return lax.dot_general(left, right, dims, preferred_element_type=f32)


def route_kernel(layer_ref, block_ref, vis_ref, row_ref, col_ref, out_ref, count_ref, blocks_ref):
    out_ref[...] = jnp.zeros_like(out_ref)

    def clear(layer, carry):
        count_ref[layer] = 0
        blocks_ref[layer * CAP] = 0
        blocks_ref[layer * CAP + 1] = 0
        return carry

    lax.fori_loop(0, LAYERS, clear, 0, unroll=8)

    def place(tile, carry):
        layer = layer_ref[tile]
        slot = count_ref[layer]
        count_ref[layer] = slot + 1
        blocks_ref[layer * CAP + slot] = block_ref[tile]
        start = layer * SENT + slot * 4
        out_ref[pl.ds(start, 2), :] = vis_ref[pl.ds(2 * tile, 2), :]
        out_ref[pl.ds(start + 2, 1), :] = row_ref[pl.ds(tile, 1), :]
        out_ref[pl.ds(start + 3, 1), :] = col_ref[pl.ds(tile, 1), :]
        return carry

    tiles = layer_ref.shape[0]
    lax.fori_loop(0, tiles, place, 0, unroll=8)
    lower = lax.broadcasted_iota(jnp.int32, (1, LANES), 1) < LANES // CAP

    def name(layer, carry):
        both = jnp.where(lower, blocks_ref[layer * CAP], blocks_ref[layer * CAP + 1])
        out_ref[pl.ds(layer * SENT + 4 * CAP, 1), :] = both.astype(f32)
        return carry

    lax.fori_loop(0, LAYERS, name, 0, unroll=8)


def grid_kernel(got_ref, twist_ref, last_ref, out_ref, patch_ref):
    rows = lax.broadcasted_iota(jnp.int32, (RB, VIS), 0).astype(f32) + 0.5
    cols = lax.broadcasted_iota(jnp.int32, (CB, VIS), 0).astype(f32) + 0.5
    empty = jnp.zeros((2 * RB, VIS), bf16)

    def one(source, slot):
        start = source * SENT + 4 * slot
        real = got_ref[pl.ds(start, 1), :]
        imag = got_ref[pl.ds(start + 1, 1), :]
        away = rows - got_ref[pl.ds(start + 2, 1), :]
        near = jnp.exp(-0.5 * (away * away))
        upper, lower = split(jnp.concatenate([near * real, near * imag], 0))
        away = cols - got_ref[pl.ds(start + 3, 1), :]
        col_upper, col_lower = split(jnp.exp(-0.5 * (away * away)))
        left = jnp.concatenate(
            [jnp.concatenate([upper, upper], 1), jnp.concatenate([lower, empty], 1)], 0
        )
        both = dot(left, jnp.concatenate([col_upper, col_lower], 1), NT)
        patch = both[: 2 * RB] + both[2 * RB :]
        row = slot * LAYERS + source
        patch_ref[pl.ds(row, RB, stride=2 * SLOTS), :] = patch[:RB]
        patch_ref[pl.ds(row + SLOTS, RB, stride=2 * SLOTS), :] = patch[RB:]

    together = 4

    def some(step, carry):
        for part in range(together):
            for slot in range(CAP):
                one(step * together + part, slot)
        return carry

    lax.fori_loop(0, LAYERS // together, some, 0)

    named = got_ref[pl.ds(4 * CAP, LAYERS, stride=SENT), :]
    source = lax.broadcasted_iota(jnp.int32, (LAYERS, SLOTS), 0)
    lane = lax.broadcasted_iota(jnp.int32, (LAYERS, SLOTS), 1)
    block = jnp.sum(
        jnp.where(source == jnp.bitwise_and(lane, LAYERS - 1), named, 0.0), 0, keepdims=True
    )
    second = block >= float(SUB)
    turn = jnp.where(second, block - float(SUB), block) * lax.broadcasted_iota(
        jnp.int32, (SUB, SLOTS), 0
    ).astype(f32)
    angle = (turn - SUB * jnp.floor(turn * (1.0 / SUB))) * (2.0 * math.pi / SUB)
    cos_all, sin_all = jnp.cos(angle), jnp.sin(angle)
    second = jnp.broadcast_to(second, (SUB, SLOTS))
    cos_part = jnp.concatenate(
        [jnp.where(second, 0.0, cos_all), jnp.where(second, cos_all, 0.0)], 0
    )
    sin_part = jnp.concatenate(
        [jnp.where(second, 0.0, sin_all), jnp.where(second, sin_all, 0.0)], 0
    )
    turns = jnp.concatenate(
        [
            jnp.concatenate([cos_part, -sin_part], 1),
            jnp.concatenate([sin_part, cos_part], 1),
        ],
        0,
    )
    turn_upper, turn_lower = split(turns)
    turn_both = jnp.concatenate([turn_upper, turn_lower], 0)
    twist_cos = twist_ref[: 2 * SUB, :]
    twist_sin = twist_ref[2 * SUB :, :]
    last_both = last_ref[...]
    last_upper = last_both[: 2 * SUB]

    for pair in range(PAIRS):
        patch = jnp.concatenate(
            [
                patch_ref[pl.ds((2 * pair + r) * 2 * SLOTS, 2 * SLOTS), :]
                for r in range(2)
            ],
            1,
        )
        patch_upper, patch_lower = split(patch)
        both = dot(turn_both, patch_upper, NN)
        along = both[: 4 * SUB] + both[4 * SUB :] + dot(turn_upper, patch_lower, NN)
        parts = []
        for r in range(2):
            real = along[: 2 * SUB, r * CB : (r + 1) * CB]
            imag = along[2 * SUB :, r * CB : (r + 1) * CB]
            parts.append(
                jnp.concatenate(
                    [real * twist_cos - imag * twist_sin, real * twist_sin + imag * twist_cos], 1
                )
            )
        upper, lower = split(jnp.concatenate(parts, 0))
        both = dot(last_both, upper, NT)
        wide = both[: 2 * SUB] + both[2 * SUB :] + dot(last_upper, lower, NT)
        for part in range(2):
            out_ref[pl.ds(2 * pair + part, PEERS, stride=2 * PAIRS), :] = wide[
                part * PEERS : (part + 1) * PEERS
            ]


def image_kernel(got_ref, upper_ref, lower_ref, cos_ref, sin_ref, out_ref, right_ref):
    group = lax.broadcasted_iota(jnp.int32, (N_SLAB, LANES), 1) // SUB
    for step in range(2 * PAIRS):
        turned = []
        for layer in range(X_CHIPS):
            value = got_ref[pl.ds(layer * N_SLAB * 2 * PAIRS + step, N_SLAB, stride=2 * PAIRS), :]
            turned.append(
                [value] + [pltpu.roll(value, SUB * shift, 1) for shift in range(1, X_CHIPS)]
            )
        parts = []
        for part in range(X_CHIPS):
            value = turned[0][(0 - part) % X_CHIPS]
            for layer in range(1, X_CHIPS):
                value = jnp.where(group == layer, turned[layer][(layer - part) % X_CHIPS], value)
            parts.append(value)
        upper, lower = split(jnp.concatenate(parts, 0))
        rows = X_CHIPS * N_SLAB
        right_ref[step * rows : (step + 1) * rows, :] = jnp.concatenate([upper, lower], 1)
    count = IMG_L // X_CHIPS
    group = lax.broadcasted_iota(jnp.int32, (count, LANES), 1) // SUB
    right = right_ref[...]
    total = None
    for part in range(X_CHIPS):
        rows = pl.ds(part * 2 * count, 2 * count)
        both = dot(upper_ref[rows, :], right, NN)
        wave_sum = both[:, :LANES] + both[:, LANES:] + dot(lower_ref[rows, :], right[:, :LANES], NN)
        lines = pl.ds(part * count, count)
        screened = wave_sum[:count] * cos_ref[lines, :] - wave_sum[count:] * sin_ref[lines, :]
        screened = screened + pltpu.roll(screened, 2 * SUB, 1)
        screened = screened + pltpu.roll(screened, SUB, 1)
        total = screened if total is None else jnp.where(group == part, screened, total)
    out_ref[...] = total


def sum_kernel(got_ref, out_ref):
    line = lax.broadcasted_iota(jnp.int32, (8, LANES), 0)
    group = lax.broadcasted_iota(jnp.int32, (8, LANES), 1) // SUB
    straight = (line // 4) == jnp.bitwise_and(line, 1)
    result = jnp.zeros((8, LANES), f32)
    for chip in range(X_CHIPS):
        total = got_ref[pl.ds(chip * 2 * Z_CHIPS, 8), :]
        for step in range(1, 2 * Z_CHIPS // 8):
            total = total + got_ref[pl.ds(chip * 2 * Z_CHIPS + 8 * step, 8), :]
        total = total + pltpu.roll(total, 4, 0)
        total = total + pltpu.roll(total, 2, 0)
        total = jnp.where(straight, total, pltpu.roll(total, 1, 0))
        for part in range(X_CHIPS):
            shift = (chip - part) % X_CHIPS
            moved = pltpu.roll(total, SUB * shift, 1) if shift else total
            chosen = (group == chip) & (jnp.bitwise_and(line, 3) == part)
            result = jnp.where(chosen, moved, result)
    out_ref[...] = result


def call(kernel, shape, specs, scratch, flops, moved):
    return pl.pallas_call(
        kernel,
        out_shape=jax.ShapeDtypeStruct(shape, f32),
        in_specs=specs,
        out_specs=VMEM,
        scratch_shapes=scratch,
        compiler_params=pltpu.CompilerParams(vmem_limit_bytes=24 * 1024 * 1024),
        cost_estimate=pl.CostEstimate(flops=flops, bytes_accessed=moved, transcendentals=0),
    )


def grid_tables():
    q = np.arange(SUB)
    c = np.arange(CB)
    sign = (1 - 2 * (q % 2))[:, None]
    twist = np.concatenate(
        [np.tile(part * sign, (2, 1)) for part in wave(q[:, None] * c[None, :], NG)], 0
    ).astype(np.float32)
    n = (4 * np.arange(N_SLAB)[None, :] + np.arange(X_CHIPS)[:, None]).reshape(-1)
    cos_part, sin_part = wave((n[:, None] - SUB // 2) * c[None, :], CB)
    last = np.concatenate(
        [
            np.concatenate([cos_part, -sin_part], 1),
            np.concatenate([sin_part, cos_part], 1),
        ],
        0,
    )
    return twist, np.concatenate(np_split(last), 0)


def image_lines():
    part, chip, half = np.meshgrid(np.arange(4), np.arange(LAYERS), np.arange(2), indexing="ij")
    return (8 * chip + 4 * half + part).reshape(-1) - IMG_L // 2


def image_tables(spread):
    pair, y, r, h, slab = np.meshgrid(
        np.arange(PAIRS), np.arange(2), np.arange(2), np.arange(2), np.arange(N_SLAB), indexing="ij"
    )
    row = (slab * ROWS_DEV + h * RB + 2 * pair + r).reshape(-1) - ROWS_DEV * N_SLAB // 2
    y = y.reshape(-1)[None, :]
    cos_part, sin_part = wave(image_lines()[:, None] * row[None, :], NG)
    real = np.where(y == 0, cos_part, -sin_part).reshape(4, -1, row.size)
    imag = np.where(y == 0, sin_part, cos_part).reshape(4, -1, row.size)
    return np_split(np.concatenate([real, imag], 1).reshape(2 * IMG_L, row.size) * spread)


def screen_tables():
    columns = IMG_M // N_SLAB
    lines = jnp.asarray(image_lines().astype(np.float32))
    lane = jnp.arange(LANES, dtype=jnp.int32)
    m_index = (
        lax.axis_index("slab") * columns
        + lax.axis_index("x") * SUB
        + jnp.bitwise_and(lane, SUB - 1)
        - IMG_M // 2
    )
    layer = ((lane // SUB) * Z_CHIPS + lax.axis_index("z")).astype(f32)
    w_value = w_reach * (2.0 * layer + 1.0 - LAYERS) / LAYERS
    l_direction = lines[:, None] * cell_size
    m_direction = m_index.astype(f32)[None, :] * cell_size
    radius = l_direction * l_direction + m_direction * m_direction
    n_lift = -radius / (1.0 + jnp.sqrt(1.0 - radius))
    phase_angle = -2.0 * math.pi * w_value[None, :] * n_lift
    return jnp.cos(phase_angle), jnp.sin(phase_angle)


def body(visibilities, row_offset, col_offset, w_layer, grid_block):
    tiles = w_layer.shape[0]
    spread = 1.0 / (
        2.0 * math.pi * kernel_width**2 * math.sqrt(tiles * LAYERS * N_SLAB * VIS)
    )
    sent = call(
        route_kernel,
        (LAYERS * SENT, VIS),
        [SMEM, SMEM, VMEM, VMEM, VMEM],
        [pltpu.SMEM((LAYERS,), jnp.int32), pltpu.SMEM((SLOTS,), jnp.int32)],
        10**6,
        5 * 10**5,
    )(w_layer, grid_block, visibilities.reshape(2 * tiles, VIS), row_offset, col_offset)
    got = lax.all_to_all(
        sent.reshape(LAYERS, 1, SENT * VIS), ("x", "z"), split_axis=0, concat_axis=0, tiled=True
    ).reshape(LAYERS * SENT, VIS)
    cos_screen, sin_screen = screen_tables()
    twist, last = grid_tables()
    pieces = call(
        grid_kernel,
        (PEERS * 2 * PAIRS, LANES),
        [VMEM] * 3,
        [pltpu.VMEM((RB * 2 * SLOTS, CB), f32)],
        10**9,
        10**6,
    )(got, jnp.asarray(twist), jnp.asarray(last))
    turned = lax.all_to_all(
        pieces.reshape(PEERS, 2 * PAIRS, LANES),
        ("x", "slab"),
        split_axis=0,
        concat_axis=0,
        tiled=True,
    ).reshape(PEERS * 2 * PAIRS, LANES)
    upper, lower = image_tables(spread)
    shares = call(
        image_kernel,
        (2 * LAYERS, LANES),
        [VMEM] * 5,
        [pltpu.VMEM((PEERS * 2 * PAIRS, 2 * LANES), bf16)],
        10**9,
        3 * 10**6,
    )(turned, jnp.asarray(upper), jnp.asarray(lower), cos_screen, sin_screen)
    got = lax.all_to_all(
        shares.reshape(LAYERS, 2, LANES), ("x", "z"), split_axis=0, concat_axis=0, tiled=True
    ).reshape(2 * LAYERS, LANES)
    return call(sum_kernel, (8, LANES), [VMEM], [], 10**5, 7 * 10**4)(got)


def solution(mesh):
    whole = ("x", "z", "slab")
    chips = Mesh(mesh.devices.reshape(X_CHIPS, Z_CHIPS, N_SLAB), whole)
    placed = (P(whole, None, None), P(whole, None), P(whole, None), P(whole), P(whole))
    return jax.shard_map(
        body, mesh=chips, in_specs=placed, out_specs=P(("x", "z"), "slab"), check_vma=False
    )
```

time: 113 us -> 93.3 us (0.83)
  the two profiles are of different devices: /device:TPU:32 before, /device:TPU:1 now
where the time goes in v2:
time: 93.3 us; the launch traced here: 92.8 us
  starting transfers between devices  29.8 us (32%)
  waiting for transfers between devices  27.9 us (30%)
  blocking collectives  17.8 us (19%)
  Pallas kernels  13.1 us (14%)
  local copies, waits for them, and re-layouts  3.04 us (3%)
  other arithmetic  1.12 us (1%)
    all_to_all x1, waiting for transfers between devices, body(): lax.all_to_all(sent.reshape(LAYERS, 1, SENT * VIS), ('x', 'z'), split_axi...  20 us
    all_to_all x1, starting transfers between devices, body(): lax.all_to_all(sent.reshape(LAYERS, 1, SENT * VIS), ('x', 'z'), split_axi...  19.2 us
    all_to_all x1, blocking collectives, body(): lax.all_to_all(shares.reshape(LAYERS, 2, LANES), ('x', 'z'), split_axis=0...  17.8 us
    all_to_all x1, starting transfers between devices, body(): lax.all_to_all(pieces.reshape(PEERS, 2 * PAIRS, LANES), ('x', 'slab'), sp...  10.5 us
    pallas_call x1, Pallas kernels, body(): call(grid_kernel, (PEERS * 2 * PAIRS, LANES), [VMEM] * 3, [pltpu.VMEM((RB...  9.5 us
    all_to_all x1, waiting for transfers between devices, body(): lax.all_to_all(pieces.reshape(PEERS, 2 * PAIRS, LANES), ('x', 'slab'), sp...  7.85 us
    unnamed x20, local copies, waits for them, and re-layouts  3.04 us
    pallas_call x1, Pallas kernels, body(): call(route_kernel, (LAYERS * SENT, VIS), [SMEM, SMEM, VMEM, VMEM, VMEM],...  1.89 us
  transfers between devices with their start and end apart: 2, of which 2 were waited for; matrix products, arithmetic and copies ran while one was open for 1% of the time, Pallas kernels for 0%

profile of v2, /device:TPU:1, one launch (start us, length us, event | category | flops | bytes accessed | tf_op | source)
XLA Modules:
  0.0 92.8 jit_solution(16935905075137398484)
XLA Ops:
  0.0 0.0 copy-start.4
  0.0 0.0 copy-start.3
  0.0 0.7 copy-done.4
  0.7 0.0 copy-done.3
  0.7 0.0 copy-start
  0.7 0.8 copy-done
  1.5 0.0 copy-start.1
  1.5 0.8 copy-done.1
  2.3 0.8 copy-done.2
  3.0 1.9 %shard_map.100 = f32[576,128]{1,0:T(8,128)} custom-call(s32[64]{0:T(128)S(1)} %copy-done.3, s32[64]{0:T(128)S(1)} %copy-done.4, f32[128,128]{1,0:T(8,128)S(1)} %bitcast.11, f32[64,128]{1,0:T(8,128)S(1)} %copy-done.1, f32[64,128]{1,0:T(8,128)S(1)} %copy-done.2), custom_call_target="tpu_custom_call" | custom-call | flops 1000000 | bytes 500000 | tf_op jit(solution)/shard_map/pallas_call | solution.py:322
  4.9 19.2 %all-to-all-start = ((f32[64,1,1152]{2,1,0:T(1,128)}), f32[64,1,1152]{2,1,0:T(1,128)S(1)}, u32[]{:S(2)}, u32[]{:S(2)}) async-start(f32[64,1,1152]{2,1,0:T(1,128)} %bitcast.1), calls=%async_computation | async-start | bytes 589824 | tf_op jit(solution)/shard_map/all_to_all | solution.py:330
  24.2 20.0 %all-to-all-done = f32[64,1,1152]{2,1,0:T(1,128)S(1)} async-done(((f32[64,1,1152]{2,1,0:T(1,128)}), f32[64,1,1152]{2,1,0:T(1,128)S(1)}, u32[]{:S(2)}, u32[]{:S(2)}) %all-to-all-start) | async-done | bytes 294944 | tf_op jit(solution)/shard_map/all_to_all | solution.py:330
  44.2 0.0 copy-done.7
  44.2 0.0 copy-done.8
  44.2 9.5 %shard_map.101 = f32[512,128]{1,0:T(8,128)} custom-call(f32[576,128]{1,0:T(8,128)S(1)} %bitcast.7, f32[128,128]{1,0:T(8,128)S(1)} %copy-done.8, bf16[128,256]{1,0:T(8,128)(2,1)S(1)} %copy-done.7), custom_call_target="tpu_custom_call" | custom-call | flops 1000000000 | bytes 1000000 | tf_op jit(solution)/shard_map/pallas_call | solution.py:335
  53.7 10.5 %all-to-all-start.1 = ((f32[32,16,128]{2,1,0:T(8,128)}), f32[32,16,128]{2,1,0:T(8,128)S(1)}, u32[]{:S(2)}, u32[]{:S(2)}) async-start(f32[32,16,128]{2,1,0:T(8,128)} %bitcast.3), calls=%async_computation.1 | async-start | bytes 524288 | tf_op jit(solution)/shard_map/all_to_all | solution.py:343
  64.3 0.0 copy-done.9
  64.3 1.1 %fusion.4 = (f32[512,128]{1,0:T(8,128)S(1)}, f32[512,128]{1,0:T(8,128)S(1)}) fusion(f32[128]{0:T(128)S(1)} %get-tuple-element.7, f32[512]{0:T(512)S(1)} %copy-done.9, f32[128]{0:T(128)S(1)} %get-tuple-element.8), kind=kLoop, calls=%fused_computation.6 | loop fusion | flops 393216 | bytes 527360 | tf_op jit(solution)/shard_map/sin | solution.py:314
  65.4 7.8 %all-to-all-done.1 = f32[32,16,128]{2,1,0:T(8,128)S(1)} async-done(((f32[32,16,128]{2,1,0:T(8,128)}), f32[32,16,128]{2,1,0:T(8,128)S(1)}, u32[]{:S(2)}, u32[]{:S(2)}) %all-to-all-start.1) | async-done | bytes 262176 | tf_op jit(solution)/shard_map/all_to_all | solution.py:343
  73.3 0.0 copy-done.6
  73.3 0.0 copy-done.5
  73.3 1.1 %shard_map.102 = f32[128,128]{1,0:T(8,128)S(1)} custom-call(f32[512,128]{1,0:T(8,128)S(1)} %bitcast.8, bf16[1024,512]{1,0:T(8,128)(2,1)S(1)} %copy-done.6, bf16[1024,512]{1,0:T(8,128)(2,1)S(1)} %copy-done.5, f32[512,128]{1,0:T(8,128)S(1)} %get-tuple-element.6.cos_ref, f32[512,128]{1,0:T(8,128)S(1)} %get-tuple-element.5.sin_ref), custom_call_target="tpu_custom_call" | custom-call | flops 1000000000 | bytes 3000000 | tf_op jit(solution)/shard_map/pallas_call | solution.py:351
  74.3 17.8 %all_to_all.15 = f32[64,2,128]{2,1,0:T(2,128)S(1)} all-to-all(f32[64,2,128]{2,1,0:T(2,128)S(1)} %bitcast.10), channel_id=1, replica_groups=mesh['x'=4,'z'=16,'slab'=8] {'x','z'}, dimensions={0} | all-to-all | bytes 131072 | tf_op jit(solution)/shard_map/all_to_all | solution.py:359
  92.1 0.7 shard_map.103
  (7 shorter events, 0.0 us)
Async XLA Ops:
  0.0 0.7 copy-start.4
  0.0 0.7 copy-start.3
  0.7 0.8 copy-start
  1.5 0.8 copy-start.1
  2.3 0.8 copy-start.2
  4.9 39.3 %copy-start.7 = (bf16[128,256]{1,0:T(8,128)(2,1)S(1)}, bf16[128,256]{1,0:T(8,128)(2,1)}, u32[]{:S(2)}) copy-start(bf16[128,256]{1,0:T(8,128)(2,1)} %constant.70.clone.last_ref) | copy-start | bytes 196612
  4.9 39.3 %copy-start.8 = (f32[128,128]{1,0:T(8,128)S(1)}, f32[128,128]{1,0:T(8,128)}, u32[]{:S(2)}) copy-start(f32[128,128]{1,0:T(8,128)} %constant.69.clone.twist_ref) | copy-start | bytes 196612
  4.9 39.3 %all-to-all-start = ((f32[64,1,1152]{2,1,0:T(1,128)}), f32[64,1,1152]{2,1,0:T(1,128)S(1)}, u32[]{:S(2)}, u32[]{:S(2)}) async-start(f32[64,1,1152]{2,1,0:T(1,128)} %bitcast.1), calls=%async_computation | async-start | bytes 589824 | tf_op jit(solution)/shard_map/all_to_all | solution.py:330
  44.2 20.1 %copy-start.9 = (f32[512]{0:T(512)S(1)}, f32[512]{0:T(512)}, u32[]{:S(2)}) copy-start(f32[512]{0:T(512)} %constant.80) | copy-start | bytes 6148
  44.2 29.0 %copy-start.6 = (bf16[1024,512]{1,0:T(8,128)(2,1)S(1)}, bf16[1024,512]{1,0:T(8,128)(2,1)}, u32[]{:S(2)}) copy-start(bf16[1024,512]{1,0:T(8,128)(2,1)} %constant.71.clone.upper_ref) | copy-start | bytes 3145732
  53.7 19.5 %copy-start.5 = (bf16[1024,512]{1,0:T(8,128)(2,1)S(1)}, bf16[1024,512]{1,0:T(8,128)(2,1)}, u32[]{:S(2)}) copy-start(bf16[1024,512]{1,0:T(8,128)(2,1)} %constant.72.clone.lower_ref) | copy-start | bytes 3145732
  53.7 19.5 %all-to-all-start.1 = ((f32[32,16,128]{2,1,0:T(8,128)}), f32[32,16,128]{2,1,0:T(8,128)S(1)}, u32[]{:S(2)}, u32[]{:S(2)}) async-start(f32[32,16,128]{2,1,0:T(8,128)} %bitcast.3), calls=%async_computation.1 | async-start | bytes 524288 | tf_op jit(solution)/shard_map/all_to_all | solution.py:343

commit v3 on v2

v3 whole, which is shorter than its diff:
```python
import math

import ml_dtypes
import numpy as np

import jax
import jax.numpy as jnp
from jax import lax
from jax.experimental import pallas as pl
from jax.experimental.pallas import tpu as pltpu
from jax.sharding import Mesh
from jax.sharding import PartitionSpec as P

NG = 4096
VIS = 128
RB = 16
CB = 128
ROWS_DEV = 32
IMG_L = 512
IMG_M = 1024
CAP = 2
LAYERS = 64
N_SLAB = 8
X_CHIPS = 4
Z_CHIPS = 16
SUB = 32
SLOTS = LAYERS * CAP
LANES = 128
SENT = 4 * CAP + 1
PEERS = X_CHIPS * N_SLAB
PAIRS = RB // 2


kernel_width = 1.0
cell_size = 2.4e-05
w_reach = 20000.0

f32 = jnp.float32
bf16 = jnp.bfloat16
VMEM = pl.BlockSpec(memory_space=pltpu.VMEM)
HBM = pl.BlockSpec(memory_space=pltpu.HBM)
NT = (((1,), (1,)), ((), ()))
NN = (((1,), (0,)), ((), ()))


def wave(turns, period):
    angle = 2.0 * np.pi * (np.asarray(turns) % period) / period
    return np.cos(angle), np.sin(angle)


def np_split(table):
    table = np.asarray(table, np.float32)
    upper = table.astype(ml_dtypes.bfloat16)
    return upper, (table - upper.astype(np.float32)).astype(ml_dtypes.bfloat16)


def split(value):
    upper = value.astype(bf16)
    return upper, (value - upper.astype(f32)).astype(bf16)


def dot(left, right, dims):
    return lax.dot_general(left, right, dims, preferred_element_type=f32)


def route_kernel(*refs):
    given, out_ref, held, (count_ref, blocks_ref, sems) = refs[:5], refs[5], refs[6:11], refs[11:]
    layer_ref, block_ref, vis_ref, row_ref, col_ref = held
    copies = [
        pltpu.make_async_copy(source, target, sems.at[index])
        for index, (source, target) in enumerate(zip(given, held))
    ]
    for copy in copies:
        copy.start()
    out_ref[...] = jnp.zeros_like(out_ref)

    def clear(layer, carry):
        count_ref[layer] = 0
        blocks_ref[layer * CAP] = 0
        blocks_ref[layer * CAP + 1] = 0
        return carry

    lax.fori_loop(0, LAYERS, clear, 0, unroll=8)
    for copy in copies:
        copy.wait()

    def place(tile, carry):
        layer = layer_ref[tile]
        slot = count_ref[layer]
        count_ref[layer] = slot + 1
        blocks_ref[layer * CAP + slot] = block_ref[tile]
        start = layer * SENT + slot * 4
        out_ref[pl.ds(start, 2), :] = vis_ref[pl.ds(2 * tile, 2), :]
        out_ref[pl.ds(start + 2, 1), :] = row_ref[pl.ds(tile, 1), :]
        out_ref[pl.ds(start + 3, 1), :] = col_ref[pl.ds(tile, 1), :]
        return carry

    tiles = layer_ref.shape[0]
    lax.fori_loop(0, tiles, place, 0, unroll=8)
    lower = lax.broadcasted_iota(jnp.int32, (1, LANES), 1) < LANES // CAP

    def name(layer, carry):
        both = jnp.where(lower, blocks_ref[layer * CAP], blocks_ref[layer * CAP + 1])
        out_ref[pl.ds(layer * SENT + 4 * CAP, 1), :] = both.astype(f32)
        return carry

    lax.fori_loop(0, LAYERS, name, 0, unroll=8)


def turn_by(value, step, period):
    real, imag = value
    step = step % period
    if 4 * step % period == 0:
        quarter = 4 * step // period
        return [(real, imag), (-imag, real), (-real, -imag), (imag, -real)][quarter]
    angle = 2.0 * math.pi * step / period
    cos_part, sin_part = math.cos(angle), math.sin(angle)
    return real * cos_part - imag * sin_part, real * sin_part + imag * cos_part


def dft(values):
    count = len(values)
    if count == 1:
        return values
    even, odd = dft(values[::2]), dft(values[1::2])
    odd = [turn_by(value, index, count) for index, value in enumerate(odd)]
    return [(a[0] + b[0], a[1] + b[1]) for a, b in zip(even, odd)] + [
        (a[0] - b[0], a[1] - b[1]) for a, b in zip(even, odd)
    ]


def grid_kernel(
    got_ref, twist_ref, last_ref, out_ref, grid_ref, upper_ref, lower_ref, name_ref, block_ref, sem
):
    named = got_ref[pl.ds(4 * CAP, LAYERS, stride=SENT), :]
    source = lax.broadcasted_iota(jnp.int32, (LAYERS, SLOTS), 0)
    lane = lax.broadcasted_iota(jnp.int32, (LAYERS, SLOTS), 1)
    name_ref[...] = jnp.sum(
        jnp.where(source == jnp.bitwise_and(lane, LAYERS - 1), named, 0.0), 0, keepdims=True
    ).astype(jnp.int32)
    copy = pltpu.make_async_copy(name_ref, block_ref, sem)
    copy.start()
    grid_ref[...] = jnp.zeros_like(grid_ref)
    offsets = jnp.concatenate(
        [got_ref[pl.ds(4 * slot + 3, LAYERS, stride=SENT), :] for slot in range(CAP)], 0
    ).T
    rows = lax.broadcasted_iota(jnp.int32, (RB, VIS), 0).astype(f32) + 0.5
    cols = lax.broadcasted_iota(jnp.int32, (VIS, CB), 1).astype(f32) + 0.5
    empty = jnp.zeros((2 * RB, VIS), bf16)
    copy.wait()

    def one(source, slot, center):
        start = source * SENT + 4 * slot
        real = got_ref[pl.ds(start, 1), :]
        imag = got_ref[pl.ds(start + 1, 1), :]
        away = rows - got_ref[pl.ds(start + 2, 1), :]
        near = jnp.exp(-0.5 * (away * away))
        upper, lower = split(jnp.concatenate([near * real, near * imag], 0))
        away = cols - center
        col_upper, col_lower = split(jnp.exp(-0.5 * (away * away)))
        left = jnp.concatenate(
            [jnp.concatenate([upper, upper], 1), jnp.concatenate([lower, empty], 1)], 0
        )
        both = dot(left, jnp.concatenate([col_upper, col_lower], 0), NN)
        grid_ref[block_ref[0, slot * LAYERS + source]] += both[: 2 * RB] + both[2 * RB :]

    together = 16

    def some(step, held):
        for part in range(together):
            for slot in range(CAP):
                lane = slot * LAYERS + part
                one(step * together + part, slot, held[:, lane : lane + 1])
        return pltpu.roll(held, SLOTS - together, 1)

    lax.fori_loop(0, LAYERS // together, some, offsets)

    wide, narrow = 8, SUB // 8
    for second in range(2):
        for low in range(wide):
            at = [second * SUB + low + wide * high for high in range(narrow)]
            turned = dft([(grid_ref[k, :RB, :], grid_ref[k, RB:, :]) for k in at])
            for index, k in enumerate(at):
                real, imag = turn_by(turned[index], index * low, SUB)
                grid_ref[k, :RB, :] = real
                grid_ref[k, RB:, :] = imag
        for low in range(narrow):
            at = [second * SUB + wide * low + high for high in range(wide)]
            turned = dft([(grid_ref[k, :RB, :], grid_ref[k, RB:, :]) for k in at])
            for index, (real, imag) in enumerate(turned):
                q = low + narrow * index
                cos_part = twist_ref[q : q + 1, :]
                sin_part = twist_ref[SUB + q : SUB + q + 1, :]
                upper, lower = split(
                    jnp.concatenate(
                        [real * cos_part - imag * sin_part, real * sin_part + imag * cos_part], 1
                    )
                )
                place = (second * SUB + q) * RB
                upper_ref[place : place + RB, :] = upper
                lower_ref[place : place + RB, :] = lower

    last_both = last_ref[...]
    last_upper = last_both[: 2 * SUB]
    for pair in range(PAIRS // 2):
        piece = slice(pair * 2 * LANES, (pair + 1) * 2 * LANES)
        both = dot(last_both, upper_ref[piece, :], NT)
        wave_sum = both[: 2 * SUB] + both[2 * SUB :] + dot(last_upper, lower_ref[piece, :], NT)
        for half in range(2):
            for part in range(2):
                row = 2 * (2 * pair + half) + part
                out_ref[pl.ds(row, PEERS, stride=2 * PAIRS), :] = wave_sum[
                    part * PEERS : (part + 1) * PEERS, half * LANES : (half + 1) * LANES
                ]


def swap_blocks(value):
    line = lax.broadcasted_iota(jnp.int32, value.shape, 0)
    block = lax.broadcasted_iota(jnp.int32, value.shape, 1) // RB
    for step in (4, 2, 1):
        line_bit = jnp.bitwise_and(line, step) != 0
        block_bit = jnp.bitwise_and(block, step) != 0
        up = pltpu.roll(pltpu.roll(value, 8 - step, 0), RB * step, 1)
        down = pltpu.roll(pltpu.roll(value, step, 0), LANES - RB * step, 1)
        moved = jnp.where(line_bit, down, up)
        value = jnp.where(line_bit == block_bit, value, moved)
    return value


def image_kernel(got_ref, upper_ref, lower_ref, cos_ref, sin_ref, out_ref, right_ref):
    blocks = SUB // N_SLAB
    for layer in range(X_CHIPS):
        for pair in range(blocks // 2):
            lines = []
            for high in (2 * pair, 2 * pair + 1):
                parts = []
                for y in range(2):
                    for h in range(2):
                        step = 2 * (h * blocks + high) + y
                        row = layer * N_SLAB * 2 * PAIRS + step
                        parts.append(
                            swap_blocks(got_ref[pl.ds(row, N_SLAB, stride=2 * PAIRS), :])
                        )
                lines.append(jnp.concatenate(parts, 1))
            upper, lower = split(jnp.concatenate(lines, 0))
            row = layer * SUB + pair * 2 * N_SLAB
            right_ref[row : row + 2 * N_SLAB, :] = upper
            right_ref[LANES + row : LANES + row + 2 * N_SLAB, :] = lower
    count = IMG_L // X_CHIPS
    group = lax.broadcasted_iota(jnp.int32, (count, LANES), 1) // SUB
    right = right_ref[...]
    total = None
    for part in range(X_CHIPS):
        rows = pl.ds(part * 2 * count, 2 * count)
        both = dot(upper_ref[rows, :], right, NT)
        wave_sum = both[:, :LANES] + both[:, LANES:] + dot(lower_ref[rows, :], right[:LANES], NT)
        lines = pl.ds(part * count, count)
        screened = wave_sum[:count] * cos_ref[lines, :] - wave_sum[count:] * sin_ref[lines, :]
        screened = screened + pltpu.roll(screened, 2 * SUB, 1)
        screened = screened + pltpu.roll(screened, SUB, 1)
        total = screened if total is None else jnp.where(group == part, screened, total)
    out_ref[...] = total


def sum_kernel(got_ref, out_ref):
    line = lax.broadcasted_iota(jnp.int32, (8, LANES), 0)
    group = lax.broadcasted_iota(jnp.int32, (8, LANES), 1) // SUB
    straight = (line // 4) == jnp.bitwise_and(line, 1)
    result = jnp.zeros((8, LANES), f32)
    for chip in range(X_CHIPS):
        total = got_ref[pl.ds(chip * 2 * Z_CHIPS, 8), :]
        for step in range(1, 2 * Z_CHIPS // 8):
            total = total + got_ref[pl.ds(chip * 2 * Z_CHIPS + 8 * step, 8), :]
        total = total + pltpu.roll(total, 4, 0)
        total = total + pltpu.roll(total, 2, 0)
        total = jnp.where(straight, total, pltpu.roll(total, 1, 0))
        for part in range(X_CHIPS):
            shift = (chip - part) % X_CHIPS
            moved = pltpu.roll(total, SUB * shift, 1) if shift else total
            chosen = (group == chip) & (jnp.bitwise_and(line, 3) == part)
            result = jnp.where(chosen, moved, result)
    out_ref[...] = result


def call(kernel, shape, specs, scratch, flops, moved, limit=24):
    return pl.pallas_call(
        kernel,
        out_shape=jax.ShapeDtypeStruct(shape, f32),
        in_specs=specs,
        out_specs=VMEM,
        scratch_shapes=scratch,
        compiler_params=pltpu.CompilerParams(vmem_limit_bytes=limit * 1024 * 1024),
        cost_estimate=pl.CostEstimate(flops=flops, bytes_accessed=moved, transcendentals=0),
    )


def grid_tables():
    q = np.arange(SUB)
    c = np.arange(CB)
    sign = (1 - 2 * (q % 2))[:, None]
    twist = np.concatenate([part * sign for part in wave(q[:, None] * c[None, :], NG)], 0)
    n = (4 * np.arange(N_SLAB)[None, :] + np.arange(X_CHIPS)[:, None]).reshape(-1)
    cos_part, sin_part = wave((n[:, None] - SUB // 2) * c[None, :], CB)
    last = np.concatenate(
        [
            np.concatenate([cos_part, -sin_part], 1),
            np.concatenate([sin_part, cos_part], 1),
        ],
        0,
    )
    return twist.astype(np.float32), np.concatenate(np_split(last), 0)


def image_lines():
    part, chip, half = np.meshgrid(np.arange(4), np.arange(LAYERS), np.arange(2), indexing="ij")
    return (8 * chip + 4 * half + part).reshape(-1) - IMG_L // 2


def image_tables(spread):
    y, h, slab, r = np.meshgrid(
        np.arange(2), np.arange(2), np.arange(N_SLAB), np.arange(RB), indexing="ij"
    )
    row = (slab * ROWS_DEV + h * RB + r).reshape(-1) - ROWS_DEV * N_SLAB // 2
    y = y.reshape(-1)[None, :]
    cos_part, sin_part = wave(image_lines()[:, None] * row[None, :], NG)
    real = np.where(y == 0, cos_part, -sin_part).reshape(4, -1, row.size)
    imag = np.where(y == 0, sin_part, cos_part).reshape(4, -1, row.size)
    return np_split(np.concatenate([real, imag], 1).reshape(2 * IMG_L, row.size) * spread)


def screen_tables():
    columns = IMG_M // N_SLAB
    lines = jnp.asarray(image_lines().astype(np.float32))
    lane = jnp.arange(LANES, dtype=jnp.int32)
    m_index = (
        lax.axis_index("slab") * columns
        + lax.axis_index("x") * SUB
        + jnp.bitwise_and(lane, SUB - 1)
        - IMG_M // 2
    )
    layer = ((lane // SUB) * Z_CHIPS + lax.axis_index("z")).astype(f32)
    w_value = w_reach * (2.0 * layer + 1.0 - LAYERS) / LAYERS
    l_direction = lines[:, None] * cell_size
    m_direction = m_index.astype(f32)[None, :] * cell_size
    radius = l_direction * l_direction + m_direction * m_direction
    n_lift = -radius / (1.0 + jnp.sqrt(1.0 - radius))
    phase_angle = -2.0 * math.pi * w_value[None, :] * n_lift
    return jnp.cos(phase_angle), jnp.sin(phase_angle)


def body(visibilities, row_offset, col_offset, w_layer, grid_block):
    tiles = w_layer.shape[0]
    spread = 1.0 / (
        2.0 * math.pi * kernel_width**2 * math.sqrt(tiles * LAYERS * N_SLAB * VIS)
    )
    sent = call(
        route_kernel,
        (LAYERS * SENT, VIS),
        [HBM] * 5,
        [
            pltpu.SMEM((tiles,), jnp.int32),
            pltpu.SMEM((tiles,), jnp.int32),
            pltpu.VMEM((2 * tiles, VIS), f32),
            pltpu.VMEM((tiles, VIS), f32),
            pltpu.VMEM((tiles, VIS), f32),
            pltpu.SMEM((LAYERS,), jnp.int32),
            pltpu.SMEM((SLOTS,), jnp.int32),
            pltpu.SemaphoreType.DMA((5,)),
        ],
        10**6,
        5 * 10**5,
        limit=60,
    )(w_layer, grid_block, visibilities.reshape(2 * tiles, VIS), row_offset, col_offset)
    got = lax.all_to_all(
        sent.reshape(LAYERS, 1, SENT * VIS), ("x", "z"), split_axis=0, concat_axis=0, tiled=True
    ).reshape(LAYERS * SENT, VIS)
    cos_screen, sin_screen = screen_tables()
    twist, last = grid_tables()
    pieces = call(
        grid_kernel,
        (PEERS * 2 * PAIRS, LANES),
        [VMEM] * 3,
        [
            pltpu.VMEM((2 * SUB, 2 * RB, CB), f32),
            pltpu.VMEM((2 * SUB * RB, 2 * CB), bf16),
            pltpu.VMEM((2 * SUB * RB, 2 * CB), bf16),
            pltpu.VMEM((1, SLOTS), jnp.int32),
            pltpu.SMEM((1, SLOTS), jnp.int32),
            pltpu.SemaphoreType.DMA,
        ],
        10**9,
        10**6,
    )(got, jnp.asarray(twist), jnp.asarray(last))
    turned = lax.all_to_all(
        pieces.reshape(PEERS, 2 * PAIRS, LANES),
        ("x", "slab"),
        split_axis=0,
        concat_axis=0,
        tiled=True,
    ).reshape(PEERS * 2 * PAIRS, LANES)
    upper, lower = image_tables(spread)
    shares = call(
        image_kernel,
        (2 * LAYERS, LANES),
        [VMEM] * 5,
        [pltpu.VMEM((2 * LANES, 2 * ROWS_DEV * N_SLAB), bf16)],
        10**9,
        3 * 10**6,
    )(turned, jnp.asarray(upper), jnp.asarray(lower), cos_screen, sin_screen)
    got = lax.all_to_all(
        shares.reshape(LAYERS, 2, LANES), ("x", "z"), split_axis=0, concat_axis=0, tiled=True
    ).reshape(2 * LAYERS, LANES)
    return call(sum_kernel, (8, LANES), [VMEM], [], 10**5, 7 * 10**4)(got)


def solution(mesh):
    whole = ("x", "z", "slab")
    chips = Mesh(mesh.devices.reshape(X_CHIPS, Z_CHIPS, N_SLAB), whole)
    placed = (P(whole, None, None), P(whole, None), P(whole, None), P(whole), P(whole))
    return jax.shard_map(
        body, mesh=chips, in_specs=placed, out_specs=P(("x", "z"), "slab"), check_vma=False
    )
```

time: 93.3 us -> 87.1 us (0.934)
  Pallas kernels: 13.1 us -> 10 us
  local copies, waits for them, and re-layouts: 3.04 us -> 0.03 us
    pallas_call x3, Pallas kernels: 12.4 us -> 9.32 us  [the longest x1 6.03 us: body(): call(grid_kernel, (PEERS * 2 * PAIRS, LANES), [VMEM] * 3, [pltpu.VMEM((2...]
    unnamed x20 -> x10, local copies, waits for them, and re-layouts: 3.04 us -> 0.03 us
where the time goes in v3:
time: 87.1 us; the launch traced here: 86.7 us
  starting transfers between devices  29.8 us (34%)
  waiting for transfers between devices  27.9 us (32%)
  blocking collectives  17.8 us (20%)
  Pallas kernels  10 us (11%)
  other arithmetic  1.12 us (1%)
    all_to_all x1, waiting for transfers between devices, body(): lax.all_to_all(sent.reshape(LAYERS, 1, SENT * VIS), ('x', 'z'), split_axi...  20 us
    all_to_all x1, starting transfers between devices, body(): lax.all_to_all(sent.reshape(LAYERS, 1, SENT * VIS), ('x', 'z'), split_axi...  19.3 us
    all_to_all x1, blocking collectives, body(): lax.all_to_all(shares.reshape(LAYERS, 2, LANES), ('x', 'z'), split_axis=0...  17.8 us
    all_to_all x1, starting transfers between devices, body(): lax.all_to_all(pieces.reshape(PEERS, 2 * PAIRS, LANES), ('x', 'slab'), sp...  10.6 us
    all_to_all x1, waiting for transfers between devices, body(): lax.all_to_all(pieces.reshape(PEERS, 2 * PAIRS, LANES), ('x', 'slab'), sp...  7.85 us
    pallas_call x1, Pallas kernels, body(): call(grid_kernel, (PEERS * 2 * PAIRS, LANES), [VMEM] * 3, [pltpu.VMEM((2...  6.03 us
    pallas_call x1, Pallas kernels, body(): call(route_kernel, (LAYERS * SENT, VIS), [HBM] * 5, [pltpu.SMEM((tiles,),...  2.07 us
  transfers between devices with their start and end apart: 2, of which 2 were waited for; matrix products, arithmetic and copies ran while one was open for 1% of the time, Pallas kernels for 0%

profile of v3, /device:TPU:1, one launch (start us, length us, event | category | flops | bytes accessed | tf_op | source)
XLA Modules:
  0.0 86.7 jit_solution(13793784485470332377)
XLA Ops:
  0.0 2.1 %shard_map.100 = f32[576,128]{1,0:T(8,128)} custom-call(s32[64]{0:T(128)} %refs_0_.1, s32[64]{0:T(128)} %refs_1_.1, f32[128,128]{1,0:T(8,128)} %bitcast.12, f32[64,128]{1,0:T(8,128)} %refs_3_.1, f32[64,128]{1,0:T(8,128)} %refs_4_.1), custom_call_target="tpu_custom_call" | custom-call | flops 1000000 | bytes 500000 | tf_op jit(solution)/shard_map/pallas_call | solution.py:356
  2.1 0.0 copy-start.2
  2.1 0.0 copy-start.3
  2.1 19.3 %all-to-all-start = ((f32[64,1,1152]{2,1,0:T(1,128)}), f32[64,1,1152]{2,1,0:T(1,128)S(1)}, u32[]{:S(2)}, u32[]{:S(2)}) async-start(f32[64,1,1152]{2,1,0:T(1,128)} %bitcast.11), calls=%async_computation | async-start | bytes 589824 | tf_op jit(solution)/shard_map/all_to_all | solution.py:374
  21.4 20.0 %all-to-all-done = f32[64,1,1152]{2,1,0:T(1,128)S(1)} async-done(((f32[64,1,1152]{2,1,0:T(1,128)}), f32[64,1,1152]{2,1,0:T(1,128)S(1)}, u32[]{:S(2)}, u32[]{:S(2)}) %all-to-all-start) | async-done | bytes 294944 | tf_op jit(solution)/shard_map/all_to_all | solution.py:374
  41.4 0.0 copy-done.2
  41.4 0.0 copy-done.3
  41.4 0.0 copy-start.4
  41.4 0.0 copy-start.1
  41.4 6.0 %shard_map.101 = f32[512,128]{1,0:T(8,128)} custom-call(f32[576,128]{1,0:T(8,128)S(1)} %bitcast.7, f32[64,128]{1,0:T(8,128)S(1)} %copy-done.3, bf16[128,256]{1,0:T(8,128)(2,1)S(1)} %copy-done.2), custom_call_target="tpu_custom_call" | custom-call | flops 1000000000 | bytes 1000000 | tf_op jit(solution)/shard_map/pallas_call | solution.py:379
  47.4 0.0 copy-start
  47.5 10.6 %all-to-all-start.1 = ((f32[32,16,128]{2,1,0:T(8,128)}), f32[32,16,128]{2,1,0:T(8,128)S(1)}, u32[]{:S(2)}, u32[]{:S(2)}) async-start(f32[32,16,128]{2,1,0:T(8,128)} %bitcast.3), calls=%async_computation.1 | async-start | bytes 524288 | tf_op jit(solution)/shard_map/all_to_all | solution.py:394
  58.0 0.0 copy-done.4
  58.1 1.1 %fusion.4 = (f32[512,128]{1,0:T(8,128)S(1)}, f32[512,128]{1,0:T(8,128)S(1)}) fusion(f32[128]{0:T(128)S(1)} %get-tuple-element.7, f32[512]{0:T(512)S(1)} %copy-done.4, f32[128]{0:T(128)S(1)} %get-tuple-element.8), kind=kLoop, calls=%fused_computation.6 | loop fusion | flops 393216 | bytes 527360 | tf_op jit(solution)/shard_map/sin | solution.py:348
  59.2 7.8 %all-to-all-done.1 = f32[32,16,128]{2,1,0:T(8,128)S(1)} async-done(((f32[32,16,128]{2,1,0:T(8,128)}), f32[32,16,128]{2,1,0:T(8,128)S(1)}, u32[]{:S(2)}, u32[]{:S(2)}) %all-to-all-start.1) | async-done | bytes 262176 | tf_op jit(solution)/shard_map/all_to_all | solution.py:394
  67.0 0.0 copy-done.1
  67.0 0.0 copy-done
  67.0 1.2 %shard_map.102 = f32[128,128]{1,0:T(8,128)S(1)} custom-call(f32[512,128]{1,0:T(8,128)S(1)} %bitcast.8, bf16[1024,512]{1,0:T(8,128)(2,1)S(1)} %copy-done.1, bf16[1024,512]{1,0:T(8,128)(2,1)S(1)} %copy-done, f32[512,128]{1,0:T(8,128)S(1)} %get-tuple-element.6.cos_ref, f32[512,128]{1,0:T(8,128)S(1)} %get-tuple-element.5.sin_ref), custom_call_target="tpu_custom_call" | custom-call | flops 1000000000 | bytes 3000000 | tf_op jit(solution)/shard_map/pallas_call | solution.py:402
  68.3 17.8 %all_to_all.15 = f32[64,2,128]{2,1,0:T(2,128)S(1)} all-to-all(f32[64,2,128]{2,1,0:T(2,128)S(1)} %bitcast.10), channel_id=1, replica_groups=mesh['x'=4,'z'=16,'slab'=8] {'x','z'}, dimensions={0} | all-to-all | bytes 131072 | tf_op jit(solution)/shard_map/all_to_all | solution.py:410
  86.0 0.7 shard_map.103
  (1 shorter events, 0.0 us)
Async XLA Ops:
  2.1 39.3 %copy-start.2 = (bf16[128,256]{1,0:T(8,128)(2,1)S(1)}, bf16[128,256]{1,0:T(8,128)(2,1)}, u32[]{:S(2)}) copy-start(bf16[128,256]{1,0:T(8,128)(2,1)} %constant.70.clone.last_ref) | copy-start | bytes 196612
  2.1 39.3 %copy-start.3 = (f32[64,128]{1,0:T(8,128)S(1)}, f32[64,128]{1,0:T(8,128)}, u32[]{:S(2)}) copy-start(f32[64,128]{1,0:T(8,128)} %constant.69.clone.twist_ref) | copy-start | bytes 98308
  2.1 39.3 %all-to-all-start = ((f32[64,1,1152]{2,1,0:T(1,128)}), f32[64,1,1152]{2,1,0:T(1,128)S(1)}, u32[]{:S(2)}, u32[]{:S(2)}) async-start(f32[64,1,1152]{2,1,0:T(1,128)} %bitcast.11), calls=%async_computation | async-start | bytes 589824 | tf_op jit(solution)/shard_map/all_to_all | solution.py:374
  41.4 16.6 %copy-start.4 = (f32[512]{0:T(512)S(1)}, f32[512]{0:T(512)}, u32[]{:S(2)}) copy-start(f32[512]{0:T(512)} %constant.80) | copy-start | bytes 6148
  41.4 25.6 %copy-start.1 = (bf16[1024,512]{1,0:T(8,128)(2,1)S(1)}, bf16[1024,512]{1,0:T(8,128)(2,1)}, u32[]{:S(2)}) copy-start(bf16[1024,512]{1,0:T(8,128)(2,1)} %constant.71.clone.upper_ref) | copy-start | bytes 3145732
  47.4 19.6 %copy-start = (bf16[1024,512]{1,0:T(8,128)(2,1)S(1)}, bf16[1024,512]{1,0:T(8,128)(2,1)}, u32[]{:S(2)}) copy-start(bf16[1024,512]{1,0:T(8,128)(2,1)} %constant.72.clone.lower_ref) | copy-start | bytes 3145732
  47.5 19.6 %all-to-all-start.1 = ((f32[32,16,128]{2,1,0:T(8,128)}), f32[32,16,128]{2,1,0:T(8,128)S(1)}, u32[]{:S(2)}, u32[]{:S(2)}) async-start(f32[32,16,128]{2,1,0:T(8,128)} %bitcast.3), calls=%async_computation.1 | async-start | bytes 524288 | tf_op jit(solution)/shard_map/all_to_all | solution.py:394

commit v4 on v3

--- a/solution.py
+++ b/solution.py
@@ -23,12 +23,17 @@
 N_SLAB = 8
 X_CHIPS = 4
 Z_CHIPS = 16
+FIRST_X = 2
+FIRST_SLAB = 4
+TILE_Z = 9
+IMAGE_Z = 8
 SUB = 32
 SLOTS = LAYERS * CAP
 LANES = 128
 SENT = 4 * CAP + 1
 PEERS = X_CHIPS * N_SLAB
 PAIRS = RB // 2
+NARROW = math.sqrt(0.5 / math.log(2.0))
 
 
 kernel_width = 1.0
@@ -143,9 +148,9 @@
     grid_ref[...] = jnp.zeros_like(grid_ref)
     offsets = jnp.concatenate(
         [got_ref[pl.ds(4 * slot + 3, LAYERS, stride=SENT), :] for slot in range(CAP)], 0
-    ).T
-    rows = lax.broadcasted_iota(jnp.int32, (RB, VIS), 0).astype(f32) + 0.5
-    cols = lax.broadcasted_iota(jnp.int32, (VIS, CB), 1).astype(f32) + 0.5
+    ).T * NARROW
+    rows = (lax.broadcasted_iota(jnp.int32, (RB, VIS), 0).astype(f32) + 0.5) * NARROW
+    cols = (lax.broadcasted_iota(jnp.int32, (VIS, CB), 1).astype(f32) + 0.5) * NARROW
     empty = jnp.zeros((2 * RB, VIS), bf16)
     copy.wait()
 
@@ -153,11 +158,11 @@
         start = source * SENT + 4 * slot
         real = got_ref[pl.ds(start, 1), :]
         imag = got_ref[pl.ds(start + 1, 1), :]
-        away = rows - got_ref[pl.ds(start + 2, 1), :]
-        near = jnp.exp(-0.5 * (away * away))
+        away = rows - got_ref[pl.ds(start + 2, 1), :] * NARROW
+        near = jnp.exp2(-(away * away))
         upper, lower = split(jnp.concatenate([near * real, near * imag], 0))
         away = cols - center
-        col_upper, col_lower = split(jnp.exp(-0.5 * (away * away)))
+        col_upper, col_lower = split(jnp.exp2(-(away * away)))
         left = jnp.concatenate(
             [jnp.concatenate([upper, upper], 1), jnp.concatenate([lower, empty], 1)], 0
         )
@@ -267,10 +272,11 @@
     group = lax.broadcasted_iota(jnp.int32, (8, LANES), 1) // SUB
     straight = (line // 4) == jnp.bitwise_and(line, 1)
     result = jnp.zeros((8, LANES), f32)
-    for chip in range(X_CHIPS):
-        total = got_ref[pl.ds(chip * 2 * Z_CHIPS, 8), :]
+    for place in range(X_CHIPS):
+        chip = (place + FIRST_X) % X_CHIPS
+        total = got_ref[pl.ds(place * 2 * Z_CHIPS, 8), :]
         for step in range(1, 2 * Z_CHIPS // 8):
-            total = total + got_ref[pl.ds(chip * 2 * Z_CHIPS + 8 * step, 8), :]
+            total = total + got_ref[pl.ds(place * 2 * Z_CHIPS + 8 * step, 8), :]
         total = total + pltpu.roll(total, 4, 0)
         total = total + pltpu.roll(total, 2, 0)
         total = jnp.where(straight, total, pltpu.roll(total, 1, 0))
@@ -299,7 +305,8 @@
     c = np.arange(CB)
     sign = (1 - 2 * (q % 2))[:, None]
     twist = np.concatenate([part * sign for part in wave(q[:, None] * c[None, :], NG)], 0)
-    n = (4 * np.arange(N_SLAB)[None, :] + np.arange(X_CHIPS)[:, None]).reshape(-1)
+    x, slab = np.divmod(column_members(), N_SLAB)
+    n = 4 * slab + x
     cos_part, sin_part = wave((n[:, None] - SUB // 2) * c[None, :], CB)
     last = np.concatenate(
         [
@@ -311,8 +318,34 @@
     return twist.astype(np.float32), np.concatenate(np_split(last), 0)
 
 
+def rotated(slow, fast, first_slow, first_fast):
+    i, j = np.meshgrid(np.arange(slow), np.arange(fast), indexing="ij")
+    return ((i + first_slow) % slow * fast + (j + first_fast) % fast).reshape(-1)
+
+
+def layer_members():
+    return rotated(X_CHIPS, Z_CHIPS, FIRST_X, TILE_Z)
+
+
+def column_members():
+    return rotated(X_CHIPS, N_SLAB, FIRST_X, FIRST_SLAB)
+
+
+def image_members():
+    return rotated(X_CHIPS, Z_CHIPS, FIRST_X, IMAGE_Z)
+
+
+def exchange(value, axes, members):
+    groups = [[int(member) for member in members]]
+    return lax.all_to_all(
+        value, axes, split_axis=0, concat_axis=0, tiled=True, axis_index_groups=groups
+    )
+
+
 def image_lines():
-    part, chip, half = np.meshgrid(np.arange(4), np.arange(LAYERS), np.arange(2), indexing="ij")
+    part, chip, half = np.meshgrid(
+        np.arange(4), image_members(), np.arange(2), indexing="ij"
+    )
     return (8 * chip + 4 * half + part).reshape(-1) - IMG_L // 2
 
 
@@ -320,6 +353,7 @@
     y, h, slab, r = np.meshgrid(
         np.arange(2), np.arange(2), np.arange(N_SLAB), np.arange(RB), indexing="ij"
     )
+    slab = (slab + FIRST_SLAB) % N_SLAB
     row = (slab * ROWS_DEV + h * RB + r).reshape(-1) - ROWS_DEV * N_SLAB // 2
     y = y.reshape(-1)[None, :]
     cos_part, sin_part = wave(image_lines()[:, None] * row[None, :], NG)
@@ -338,7 +372,8 @@
         + jnp.bitwise_and(lane, SUB - 1)
         - IMG_M // 2
     )
-    layer = ((lane // SUB) * Z_CHIPS + lax.axis_index("z")).astype(f32)
+    place = (lax.axis_index("z") + Z_CHIPS - TILE_Z) % Z_CHIPS
+    layer = ((lane // SUB) * Z_CHIPS + place).astype(f32)
     w_value = w_reach * (2.0 * layer + 1.0 - LAYERS) / LAYERS
     l_direction = lines[:, None] * cell_size
     m_direction = m_index.astype(f32)[None, :] * cell_size
@@ -371,9 +406,8 @@
         5 * 10**5,
         limit=60,
     )(w_layer, grid_block, visibilities.reshape(2 * tiles, VIS), row_offset, col_offset)
-    got = lax.all_to_all(
-        sent.reshape(LAYERS, 1, SENT * VIS), ("x", "z"), split_axis=0, concat_axis=0, tiled=True
-    ).reshape(LAYERS * SENT, VIS)
+    got = exchange(sent.reshape(LAYERS, 1, SENT * VIS), ("x", "z"), layer_members())
+    got = got.reshape(LAYERS * SENT, VIS)
     cos_screen, sin_screen = screen_tables()
     twist, last = grid_tables()
     pieces = call(
@@ -391,12 +425,8 @@
         10**9,
         10**6,
     )(got, jnp.asarray(twist), jnp.asarray(last))
-    turned = lax.all_to_all(
-        pieces.reshape(PEERS, 2 * PAIRS, LANES),
-        ("x", "slab"),
-        split_axis=0,
-        concat_axis=0,
-        tiled=True,
+    turned = exchange(
+        pieces.reshape(PEERS, 2 * PAIRS, LANES), ("x", "slab"), column_members()
     ).reshape(PEERS * 2 * PAIRS, LANES)
     upper, lower = image_tables(spread)
     shares = call(
@@ -407,9 +437,8 @@
         10**9,
         3 * 10**6,
     )(turned, jnp.asarray(upper), jnp.asarray(lower), cos_screen, sin_screen)
-    got = lax.all_to_all(
-        shares.reshape(LAYERS, 2, LANES), ("x", "z"), split_axis=0, concat_axis=0, tiled=True
-    ).reshape(2 * LAYERS, LANES)
+    got = exchange(shares.reshape(LAYERS, 2, LANES), ("x", "z"), image_members())
+    got = got.reshape(2 * LAYERS, LANES)
     return call(sum_kernel, (8, LANES), [VMEM], [], 10**5, 7 * 10**4)(got)
 
 

time: 87.1 us -> 78.1 us (0.90)
  waiting for transfers between devices: 27.9 us -> 16.8 us
  starting transfers between devices: 29.8 us -> 32.1 us
    all_to_all x2, waiting for transfers between devices: 27.9 us -> 16.8 us  [exchange(): lax.all_to_all(value, axes, split_axis=0, concat_axis=0, tiled=True, axis...]
    all_to_all x2, starting transfers between devices: 29.8 us -> 32.1 us  [exchange(): lax.all_to_all(value, axes, split_axis=0, concat_axis=0, tiled=True, axis...]
where the time goes in v4:
time: 78.1 us; the launch traced here: 77.2 us
  starting transfers between devices  32.1 us (41%)
  blocking collectives  17.2 us (22%)
  waiting for transfers between devices  16.8 us (22%)
  Pallas kernels  9.9 us (13%)
  other arithmetic  1.11 us (1%)
    all_to_all x2, starting transfers between devices, exchange(): lax.all_to_all(value, axes, split_axis=0, concat_axis=0, tiled=True, axis...  32.1 us
    all_to_all x1, blocking collectives, exchange(): lax.all_to_all(value, axes, split_axis=0, concat_axis=0, tiled=True, axis...  17.2 us
    all_to_all x2, waiting for transfers between devices, exchange(): lax.all_to_all(value, axes, split_axis=0, concat_axis=0, tiled=True, axis...  16.8 us
    pallas_call x1, Pallas kernels, body(): call(grid_kernel, (PEERS * 2 * PAIRS, LANES), [VMEM] * 3, [pltpu.VMEM((2...  5.92 us
    pallas_call x1, Pallas kernels, body(): call(route_kernel, (LAYERS * SENT, VIS), [HBM] * 5, [pltpu.SMEM((tiles,),...  2.07 us
  transfers between devices with their start and end apart: 2, of which 2 were waited for; matrix products, arithmetic and copies ran while one was open for 1% of the time, Pallas kernels for 0%

profile of v4, /device:TPU:1, one launch (start us, length us, event | category | flops | bytes accessed | tf_op | source)
XLA Modules:
  0.0 77.2 jit_solution(14911036513095343265)
XLA Ops:
  0.0 2.1 %shard_map.100 = f32[576,128]{1,0:T(8,128)} custom-call(s32[64]{0:T(128)} %refs_0_.1, s32[64]{0:T(128)} %refs_1_.1, f32[128,128]{1,0:T(8,128)} %bitcast.12, f32[64,128]{1,0:T(8,128)} %refs_3_.1, f32[64,128]{1,0:T(8,128)} %refs_4_.1), custom_call_target="tpu_custom_call" | custom-call | flops 1000000 | bytes 500000 | tf_op jit(solution)/shard_map/pallas_call | solution.py:391
  2.1 0.0 copy-start.2
  2.1 22.1 %all-to-all-start = ((f32[64,1,1152]{2,1,0:T(1,128)}), f32[64,1,1152]{2,1,0:T(1,128)S(1)}, u32[]{:S(2)}, u32[]{:S(2)}) async-start(f32[64,1,1152]{2,1,0:T(1,128)} %bitcast.11), calls=%async_computation | async-start | bytes 589824 | tf_op jit(solution)/shard_map/all_to_all | solution.py:340
  24.3 0.0 copy-start.3
  24.3 13.8 %all-to-all-done = f32[64,1,1152]{2,1,0:T(1,128)S(1)} async-done(((f32[64,1,1152]{2,1,0:T(1,128)}), f32[64,1,1152]{2,1,0:T(1,128)S(1)}, u32[]{:S(2)}, u32[]{:S(2)}) %all-to-all-start) | async-done | bytes 294944 | tf_op jit(solution)/shard_map/all_to_all | solution.py:340
  38.1 0.0 copy-done.2
  38.1 0.0 copy-done.3
  38.1 0.0 copy-start.4
  38.1 0.0 copy-start.1
  38.1 5.9 %shard_map.101 = f32[512,128]{1,0:T(8,128)} custom-call(f32[576,128]{1,0:T(8,128)S(1)} %bitcast.7, f32[64,128]{1,0:T(8,128)S(1)} %copy-done.3, bf16[128,256]{1,0:T(8,128)(2,1)S(1)} %copy-done.2), custom_call_target="tpu_custom_call" | custom-call | flops 1000000000 | bytes 1000000 | tf_op jit(solution)/shard_map/pallas_call | solution.py:413
  44.1 0.0 copy-start
  44.1 9.9 %all-to-all-start.1 = ((f32[32,16,128]{2,1,0:T(8,128)}), f32[32,16,128]{2,1,0:T(8,128)S(1)}, u32[]{:S(2)}, u32[]{:S(2)}) async-start(f32[32,16,128]{2,1,0:T(8,128)} %bitcast.3), calls=%async_computation.1 | async-start | bytes 524288 | tf_op jit(solution)/shard_map/all_to_all | solution.py:340
  54.0 0.0 copy-done.4
  54.0 1.1 %fusion.4 = (f32[512,128]{1,0:T(8,128)S(1)}, f32[512,128]{1,0:T(8,128)S(1)}) fusion(f32[128]{0:T(128)S(1)} %get-tuple-element.7, f32[512]{0:T(512)S(1)} %copy-done.4, f32[128]{0:T(128)S(1)} %get-tuple-element.8), kind=kLoop, calls=%fused_computation.6 | loop fusion | flops 393216 | bytes 527360 | tf_op jit(solution)/shard_map/sin | solution.py:383
  55.1 2.9 %all-to-all-done.1 = f32[32,16,128]{2,1,0:T(8,128)S(1)} async-done(((f32[32,16,128]{2,1,0:T(8,128)}), f32[32,16,128]{2,1,0:T(8,128)S(1)}, u32[]{:S(2)}, u32[]{:S(2)}) %all-to-all-start.1) | async-done | bytes 262176 | tf_op jit(solution)/shard_map/all_to_all | solution.py:340
  58.1 0.0 copy-done.1
  58.1 0.0 copy-done
  58.1 1.2 %shard_map.102 = f32[128,128]{1,0:T(8,128)S(1)} custom-call(f32[512,128]{1,0:T(8,128)S(1)} %bitcast.8, bf16[1024,512]{1,0:T(8,128)(2,1)S(1)} %copy-done.1, bf16[1024,512]{1,0:T(8,128)(2,1)S(1)} %copy-done, f32[512,128]{1,0:T(8,128)S(1)} %get-tuple-element.6.cos_ref, f32[512,128]{1,0:T(8,128)S(1)} %get-tuple-element.5.sin_ref), custom_call_target="tpu_custom_call" | custom-call | flops 1000000000 | bytes 3000000 | tf_op jit(solution)/shard_map/pallas_call | solution.py:432
  59.3 17.2 %all_to_all.15 = f32[64,2,128]{2,1,0:T(2,128)S(1)} all-to-all(f32[64,2,128]{2,1,0:T(2,128)S(1)} %bitcast.10), channel_id=1, replica_groups={{320,328,336,344,352,360,368,376,256,264,272,280,288,296,304,312,448,45..., dimensions={0} | all-to-all | bytes 131072 | tf_op jit(solution)/shard_map/all_to_all | solution.py:340
  76.5 0.7 shard_map.103
  (1 shorter events, 0.0 us)
Async XLA Ops:
  2.1 36.0 %copy-start.2 = (bf16[128,256]{1,0:T(8,128)(2,1)S(1)}, bf16[128,256]{1,0:T(8,128)(2,1)}, u32[]{:S(2)}) copy-start(bf16[128,256]{1,0:T(8,128)(2,1)} %constant.85.clone.last_ref) | copy-start | bytes 196612
  2.1 36.0 %all-to-all-start = ((f32[64,1,1152]{2,1,0:T(1,128)}), f32[64,1,1152]{2,1,0:T(1,128)S(1)}, u32[]{:S(2)}, u32[]{:S(2)}) async-start(f32[64,1,1152]{2,1,0:T(1,128)} %bitcast.11), calls=%async_computation | async-start | bytes 589824 | tf_op jit(solution)/shard_map/all_to_all | solution.py:340
  24.3 13.9 %copy-start.3 = (f32[64,128]{1,0:T(8,128)S(1)}, f32[64,128]{1,0:T(8,128)}, u32[]{:S(2)}) copy-start(f32[64,128]{1,0:T(8,128)} %constant.84.clone.twist_ref) | copy-start | bytes 98308
  38.1 15.9 %copy-start.4 = (f32[512]{0:T(512)S(1)}, f32[512]{0:T(512)}, u32[]{:S(2)}) copy-start(f32[512]{0:T(512)} %constant.95) | copy-start | bytes 6148
  38.1 19.9 %copy-start.1 = (bf16[1024,512]{1,0:T(8,128)(2,1)S(1)}, bf16[1024,512]{1,0:T(8,128)(2,1)}, u32[]{:S(2)}) copy-start(bf16[1024,512]{1,0:T(8,128)(2,1)} %constant.86.clone.upper_ref) | copy-start | bytes 3145732
  44.1 14.0 %copy-start = (bf16[1024,512]{1,0:T(8,128)(2,1)S(1)}, bf16[1024,512]{1,0:T(8,128)(2,1)}, u32[]{:S(2)}) copy-start(bf16[1024,512]{1,0:T(8,128)(2,1)} %constant.87.clone.lower_ref) | copy-start | bytes 3145732
  44.1 14.0 %all-to-all-start.1 = ((f32[32,16,128]{2,1,0:T(8,128)}), f32[32,16,128]{2,1,0:T(8,128)S(1)}, u32[]{:S(2)}, u32[]{:S(2)}) async-start(f32[32,16,128]{2,1,0:T(8,128)} %bitcast.3), calls=%async_computation.1 | async-start | bytes 524288 | tf_op jit(solution)/shard_map/all_to_all | solution.py:340

commit v5 on v4

--- a/solution.py
+++ b/solution.py
@@ -69,7 +69,7 @@
 
 
 def route_kernel(*refs):
-    given, out_ref, held, (count_ref, blocks_ref, sems) = refs[:5], refs[5], refs[6:11], refs[11:]
+    given, out_ref, held, (count_ref, sems) = refs[:5], refs[5], refs[6:11], refs[11:]
     layer_ref, block_ref, vis_ref, row_ref, col_ref = held
     copies = [
         pltpu.make_async_copy(source, target, sems.at[index])
@@ -81,35 +81,27 @@
 
     def clear(layer, carry):
         count_ref[layer] = 0
-        blocks_ref[layer * CAP] = 0
-        blocks_ref[layer * CAP + 1] = 0
         return carry
 
-    lax.fori_loop(0, LAYERS, clear, 0, unroll=8)
+    lax.fori_loop(0, LAYERS, clear, 0, unroll=16)
     for copy in copies:
         copy.wait()
+    part = lax.broadcasted_iota(jnp.int32, (1, LANES), 1) // (LANES // CAP)
 
     def place(tile, carry):
         layer = layer_ref[tile]
         slot = count_ref[layer]
         count_ref[layer] = slot + 1
-        blocks_ref[layer * CAP + slot] = block_ref[tile]
         start = layer * SENT + slot * 4
         out_ref[pl.ds(start, 2), :] = vis_ref[pl.ds(2 * tile, 2), :]
         out_ref[pl.ds(start + 2, 1), :] = row_ref[pl.ds(tile, 1), :]
         out_ref[pl.ds(start + 3, 1), :] = col_ref[pl.ds(tile, 1), :]
+        named = out_ref.at[pl.ds(layer * SENT + 4 * CAP, 1), :]
+        block = jnp.full((1, LANES), block_ref[tile], jnp.int32).astype(f32)
+        pltpu.store(named, block, mask=part == slot)
         return carry
 
-    tiles = layer_ref.shape[0]
-    lax.fori_loop(0, tiles, place, 0, unroll=8)
-    lower = lax.broadcasted_iota(jnp.int32, (1, LANES), 1) < LANES // CAP
-
-    def name(layer, carry):
-        both = jnp.where(lower, blocks_ref[layer * CAP], blocks_ref[layer * CAP + 1])
-        out_ref[pl.ds(layer * SENT + 4 * CAP, 1), :] = both.astype(f32)
-        return carry
-
-    lax.fori_loop(0, LAYERS, name, 0, unroll=8)
+    lax.fori_loop(0, layer_ref.shape[0], place, 0, unroll=16)
 
 
 def turn_by(value, step, period):
@@ -151,7 +143,6 @@
     ).T * NARROW
     rows = (lax.broadcasted_iota(jnp.int32, (RB, VIS), 0).astype(f32) + 0.5) * NARROW
     cols = (lax.broadcasted_iota(jnp.int32, (VIS, CB), 1).astype(f32) + 0.5) * NARROW
-    empty = jnp.zeros((2 * RB, VIS), bf16)
     copy.wait()
 
     def one(source, slot, center):
@@ -163,11 +154,10 @@
         upper, lower = split(jnp.concatenate([near * real, near * imag], 0))
         away = cols - center
         col_upper, col_lower = split(jnp.exp2(-(away * away)))
-        left = jnp.concatenate(
-            [jnp.concatenate([upper, upper], 1), jnp.concatenate([lower, empty], 1)], 0
-        )
-        both = dot(left, jnp.concatenate([col_upper, col_lower], 0), NN)
-        grid_ref[block_ref[0, slot * LAYERS + source]] += both[: 2 * RB] + both[2 * RB :]
+        left = jnp.concatenate([upper, lower], 0)
+        both = dot(left, jnp.concatenate([col_upper, col_lower], 1), NN)
+        patch = both[:, :CB] + both[:, CB:]
+        grid_ref[block_ref[0, slot * LAYERS + source]] += patch[: 2 * RB] + patch[2 * RB :]
 
     together = 16
 
@@ -399,7 +389,6 @@
             pltpu.VMEM((tiles, VIS), f32),
             pltpu.VMEM((tiles, VIS), f32),
             pltpu.SMEM((LAYERS,), jnp.int32),
-            pltpu.SMEM((SLOTS,), jnp.int32),
             pltpu.SemaphoreType.DMA((5,)),
         ],
         10**6,

time: 78.1 us -> 77.9 us (level)
  no operation moved by 1% of the time
where the time goes in v5:
time: 77.9 us; the launch traced here: 77.1 us
  starting transfers between devices  32 us (41%)
  blocking collectives  17.3 us (22%)
  waiting for transfers between devices  16.8 us (22%)
  Pallas kernels  9.72 us (12%)
  other arithmetic  1.11 us (1%)
    all_to_all x2, starting transfers between devices, exchange(): lax.all_to_all(value, axes, split_axis=0, concat_axis=0, tiled=True, axis...  32 us
    all_to_all x1, blocking collectives, exchange(): lax.all_to_all(value, axes, split_axis=0, concat_axis=0, tiled=True, axis...  17.3 us
    all_to_all x2, waiting for transfers between devices, exchange(): lax.all_to_all(value, axes, split_axis=0, concat_axis=0, tiled=True, axis...  16.8 us
    pallas_call x1, Pallas kernels, body(): call(grid_kernel, (PEERS * 2 * PAIRS, LANES), [VMEM] * 3, [pltpu.VMEM((2...  5.92 us
    pallas_call x1, Pallas kernels, body(): call(route_kernel, (LAYERS * SENT, VIS), [HBM] * 5, [pltpu.SMEM((tiles,),...  1.89 us
  transfers between devices with their start and end apart: 2, of which 2 were waited for; matrix products, arithmetic and copies ran while one was open for 1% of the time, Pallas kernels for 0%

profile of v5, /device:TPU:1, one launch (start us, length us, event | category | flops | bytes accessed | tf_op | source)
XLA Modules:
  0.0 77.1 jit_solution(12080161608863356520)
XLA Ops:
  0.0 1.9 %shard_map.100 = f32[576,128]{1,0:T(8,128)} custom-call(s32[64]{0:T(128)} %refs_0_.1, s32[64]{0:T(128)} %refs_1_.1, f32[128,128]{1,0:T(8,128)} %bitcast.12, f32[64,128]{1,0:T(8,128)} %refs_3_.1, f32[64,128]{1,0:T(8,128)} %refs_4_.1), custom_call_target="tpu_custom_call" | custom-call | flops 1000000 | bytes 500000 | tf_op jit(solution)/shard_map/pallas_call | solution.py:381
  1.9 0.0 copy-start.2
  1.9 22.1 %all-to-all-start = ((f32[64,1,1152]{2,1,0:T(1,128)}), f32[64,1,1152]{2,1,0:T(1,128)S(1)}, u32[]{:S(2)}, u32[]{:S(2)}) async-start(f32[64,1,1152]{2,1,0:T(1,128)} %bitcast.11), calls=%async_computation | async-start | bytes 589824 | tf_op jit(solution)/shard_map/all_to_all | solution.py:330
  24.1 0.0 copy-start.3
  24.1 13.8 %all-to-all-done = f32[64,1,1152]{2,1,0:T(1,128)S(1)} async-done(((f32[64,1,1152]{2,1,0:T(1,128)}), f32[64,1,1152]{2,1,0:T(1,128)S(1)}, u32[]{:S(2)}, u32[]{:S(2)}) %all-to-all-start) | async-done | bytes 294944 | tf_op jit(solution)/shard_map/all_to_all | solution.py:330
  37.9 0.0 copy-done.2
  37.9 0.0 copy-done.3
  37.9 0.0 copy-start.4
  38.0 0.0 copy-start.1
  38.0 5.9 %shard_map.101 = f32[512,128]{1,0:T(8,128)} custom-call(f32[576,128]{1,0:T(8,128)S(1)} %bitcast.7, f32[64,128]{1,0:T(8,128)S(1)} %copy-done.3, bf16[128,256]{1,0:T(8,128)(2,1)S(1)} %copy-done.2), custom_call_target="tpu_custom_call" | custom-call | flops 1000000000 | bytes 1000000 | tf_op jit(solution)/shard_map/pallas_call | solution.py:402
  43.9 0.0 copy-start
  43.9 9.9 %all-to-all-start.1 = ((f32[32,16,128]{2,1,0:T(8,128)}), f32[32,16,128]{2,1,0:T(8,128)S(1)}, u32[]{:S(2)}, u32[]{:S(2)}) async-start(f32[32,16,128]{2,1,0:T(8,128)} %bitcast.3), calls=%async_computation.1 | async-start | bytes 524288 | tf_op jit(solution)/shard_map/all_to_all | solution.py:330
  53.8 0.0 copy-done.4
  53.8 1.1 %fusion.4 = (f32[512,128]{1,0:T(8,128)S(1)}, f32[512,128]{1,0:T(8,128)S(1)}) fusion(f32[128]{0:T(128)S(1)} %get-tuple-element.7, f32[512]{0:T(512)S(1)} %copy-done.4, f32[128]{0:T(128)S(1)} %get-tuple-element.8), kind=kLoop, calls=%fused_computation.6 | loop fusion | flops 393216 | bytes 527360 | tf_op jit(solution)/shard_map/sin | solution.py:373
  54.9 2.9 %all-to-all-done.1 = f32[32,16,128]{2,1,0:T(8,128)S(1)} async-done(((f32[32,16,128]{2,1,0:T(8,128)}), f32[32,16,128]{2,1,0:T(8,128)S(1)}, u32[]{:S(2)}, u32[]{:S(2)}) %all-to-all-start.1) | async-done | bytes 262176 | tf_op jit(solution)/shard_map/all_to_all | solution.py:330
  57.9 0.0 copy-done.1
  57.9 0.0 copy-done
  57.9 1.2 %shard_map.102 = f32[128,128]{1,0:T(8,128)S(1)} custom-call(f32[512,128]{1,0:T(8,128)S(1)} %bitcast.8, bf16[1024,512]{1,0:T(8,128)(2,1)S(1)} %copy-done.1, bf16[1024,512]{1,0:T(8,128)(2,1)S(1)} %copy-done, f32[512,128]{1,0:T(8,128)S(1)} %get-tuple-element.6.cos_ref, f32[512,128]{1,0:T(8,128)S(1)} %get-tuple-element.5.sin_ref), custom_call_target="tpu_custom_call" | custom-call | flops 1000000000 | bytes 3000000 | tf_op jit(solution)/shard_map/pallas_call | solution.py:421
  59.1 17.3 %all_to_all.15 = f32[64,2,128]{2,1,0:T(2,128)S(1)} all-to-all(f32[64,2,128]{2,1,0:T(2,128)S(1)} %bitcast.10), channel_id=1, replica_groups={{320,328,336,344,352,360,368,376,256,264,272,280,288,296,304,312,448,45..., dimensions={0} | all-to-all | bytes 131072 | tf_op jit(solution)/shard_map/all_to_all | solution.py:330
  76.4 0.7 shard_map.103
  (1 shorter events, 0.0 us)
Async XLA Ops:
  1.9 36.0 %copy-start.2 = (bf16[128,256]{1,0:T(8,128)(2,1)S(1)}, bf16[128,256]{1,0:T(8,128)(2,1)}, u32[]{:S(2)}) copy-start(bf16[128,256]{1,0:T(8,128)(2,1)} %constant.85.clone.last_ref) | copy-start | bytes 196612
  1.9 36.0 %all-to-all-start = ((f32[64,1,1152]{2,1,0:T(1,128)}), f32[64,1,1152]{2,1,0:T(1,128)S(1)}, u32[]{:S(2)}, u32[]{:S(2)}) async-start(f32[64,1,1152]{2,1,0:T(1,128)} %bitcast.11), calls=%async_computation | async-start | bytes 589824 | tf_op jit(solution)/shard_map/all_to_all | solution.py:330
  24.1 13.9 %copy-start.3 = (f32[64,128]{1,0:T(8,128)S(1)}, f32[64,128]{1,0:T(8,128)}, u32[]{:S(2)}) copy-start(f32[64,128]{1,0:T(8,128)} %constant.84.clone.twist_ref) | copy-start | bytes 98308
  37.9 15.9 %copy-start.4 = (f32[512]{0:T(512)S(1)}, f32[512]{0:T(512)}, u32[]{:S(2)}) copy-start(f32[512]{0:T(512)} %constant.95) | copy-start | bytes 6148
  38.0 19.9 %copy-start.1 = (bf16[1024,512]{1,0:T(8,128)(2,1)S(1)}, bf16[1024,512]{1,0:T(8,128)(2,1)}, u32[]{:S(2)}) copy-start(bf16[1024,512]{1,0:T(8,128)(2,1)} %constant.86.clone.upper_ref) | copy-start | bytes 3145732
  43.9 14.0 %copy-start = (bf16[1024,512]{1,0:T(8,128)(2,1)S(1)}, bf16[1024,512]{1,0:T(8,128)(2,1)}, u32[]{:S(2)}) copy-start(bf16[1024,512]{1,0:T(8,128)(2,1)} %constant.87.clone.lower_ref) | copy-start | bytes 3145732
  43.9 14.0 %all-to-all-start.1 = ((f32[32,16,128]{2,1,0:T(8,128)}), f32[32,16,128]{2,1,0:T(8,128)S(1)}, u32[]{:S(2)}, u32[]{:S(2)}) async-start(f32[32,16,128]{2,1,0:T(8,128)} %bitcast.3), calls=%async_computation.1 | async-start | bytes 524288 | tf_op jit(solution)/shard_map/all_to_all | solution.py:330

commit v6 on v5

--- a/solution.py
+++ b/solution.py
@@ -94,8 +94,8 @@
         count_ref[layer] = slot + 1
         start = layer * SENT + slot * 4
         out_ref[pl.ds(start, 2), :] = vis_ref[pl.ds(2 * tile, 2), :]
-        out_ref[pl.ds(start + 2, 1), :] = row_ref[pl.ds(tile, 1), :]
-        out_ref[pl.ds(start + 3, 1), :] = col_ref[pl.ds(tile, 1), :]
+        out_ref[pl.ds(start + 2, 1), :] = row_ref[pl.ds(tile, 1), :] * NARROW
+        out_ref[pl.ds(start + 3, 1), :] = col_ref[pl.ds(tile, 1), :] * NARROW
         named = out_ref.at[pl.ds(layer * SENT + 4 * CAP, 1), :]
         block = jnp.full((1, LANES), block_ref[tile], jnp.int32).astype(f32)
         pltpu.store(named, block, mask=part == slot)
@@ -138,37 +138,32 @@
     copy = pltpu.make_async_copy(name_ref, block_ref, sem)
     copy.start()
     grid_ref[...] = jnp.zeros_like(grid_ref)
-    offsets = jnp.concatenate(
-        [got_ref[pl.ds(4 * slot + 3, LAYERS, stride=SENT), :] for slot in range(CAP)], 0
-    ).T * NARROW
     rows = (lax.broadcasted_iota(jnp.int32, (RB, VIS), 0).astype(f32) + 0.5) * NARROW
-    cols = (lax.broadcasted_iota(jnp.int32, (VIS, CB), 1).astype(f32) + 0.5) * NARROW
+    cols = (lax.broadcasted_iota(jnp.int32, (CB, VIS), 0).astype(f32) + 0.5) * NARROW
     copy.wait()
 
-    def one(source, slot, center):
+    def one(source, slot):
         start = source * SENT + 4 * slot
         real = got_ref[pl.ds(start, 1), :]
         imag = got_ref[pl.ds(start + 1, 1), :]
-        away = rows - got_ref[pl.ds(start + 2, 1), :] * NARROW
+        away = rows - got_ref[pl.ds(start + 2, 1), :]
         near = jnp.exp2(-(away * away))
         upper, lower = split(jnp.concatenate([near * real, near * imag], 0))
-        away = cols - center
+        away = cols - got_ref[pl.ds(start + 3, 1), :]
         col_upper, col_lower = split(jnp.exp2(-(away * away)))
-        left = jnp.concatenate([upper, lower], 0)
-        both = dot(left, jnp.concatenate([col_upper, col_lower], 1), NN)
-        patch = both[:, :CB] + both[:, CB:]
-        grid_ref[block_ref[0, slot * LAYERS + source]] += patch[: 2 * RB] + patch[2 * RB :]
+        left = jnp.concatenate([upper, lower, upper], 1)
+        right = jnp.concatenate([col_upper, col_upper, col_lower], 1)
+        grid_ref[block_ref[0, slot * LAYERS + source]] += dot(left, right, NT)
 
     together = 16
 
-    def some(step, held):
+    def some(step, carry):
         for part in range(together):
             for slot in range(CAP):
-                lane = slot * LAYERS + part
-                one(step * together + part, slot, held[:, lane : lane + 1])
-        return pltpu.roll(held, SLOTS - together, 1)
-
-    lax.fori_loop(0, LAYERS // together, some, offsets)
+                one(step * together + part, slot)
+        return carry
+
+    lax.fori_loop(0, LAYERS // together, some, 0)
 
     wide, narrow = 8, SUB // 8
     for second in range(2):
@@ -278,10 +273,10 @@
     out_ref[...] = result
 
 
-def call(kernel, shape, specs, scratch, flops, moved, limit=24):
+def call(kernel, shape, specs, scratch, flops, moved, limit=24, out=jax.ShapeDtypeStruct):
     return pl.pallas_call(
         kernel,
-        out_shape=jax.ShapeDtypeStruct(shape, f32),
+        out_shape=out(shape, f32),
         in_specs=specs,
         out_specs=VMEM,
         scratch_shapes=scratch,
@@ -394,6 +389,7 @@
         10**6,
         5 * 10**5,
         limit=60,
+        out=pltpu.VMEM,
     )(w_layer, grid_block, visibilities.reshape(2 * tiles, VIS), row_offset, col_offset)
     got = exchange(sent.reshape(LAYERS, 1, SENT * VIS), ("x", "z"), layer_members())
     got = got.reshape(LAYERS * SENT, VIS)
@@ -413,6 +409,7 @@
         ],
         10**9,
         10**6,
+        out=pltpu.VMEM,
     )(got, jnp.asarray(twist), jnp.asarray(last))
     turned = exchange(
         pieces.reshape(PEERS, 2 * PAIRS, LANES), ("x", "slab"), column_members()

time: 77.9 us -> 79 us (1.014)
  Pallas kernels: 9.72 us -> 10.8 us
    pallas_call x1, Pallas kernels: 5.92 us -> 7.04 us  [body(): call(grid_kernel, (PEERS * 2 * PAIRS, LANES), [VMEM] * 3, [pltpu.VMEM((2...]
where the time goes in v6:
time: 79 us; the launch traced here: 78.1 us
  starting transfers between devices  32 us (41%)
  blocking collectives  17.3 us (22%)
  waiting for transfers between devices  16.8 us (21%)
  Pallas kernels  10.8 us (14%)
  other arithmetic  1.11 us (1%)
    all_to_all x2, starting transfers between devices, exchange(): lax.all_to_all(value, axes, split_axis=0, concat_axis=0, tiled=True, axis...  32 us
    all_to_all x1, blocking collectives, exchange(): lax.all_to_all(value, axes, split_axis=0, concat_axis=0, tiled=True, axis...  17.3 us
    all_to_all x2, waiting for transfers between devices, exchange(): lax.all_to_all(value, axes, split_axis=0, concat_axis=0, tiled=True, axis...  16.8 us
    pallas_call x1, Pallas kernels, body(): call(grid_kernel, (PEERS * 2 * PAIRS, LANES), [VMEM] * 3, [pltpu.VMEM((2...  7.04 us
    pallas_call x1, Pallas kernels, body(): call(route_kernel, (LAYERS * SENT, VIS), [HBM] * 5, [pltpu.SMEM((tiles,),...  1.89 us
  transfers between devices with their start and end apart: 2, of which 2 were waited for; matrix products, arithmetic and copies ran while one was open for 1% of the time, Pallas kernels for 0%

profile of v6, /device:TPU:1, one launch (start us, length us, event | category | flops | bytes accessed | tf_op | source)
XLA Modules:
  0.0 78.1 jit_solution(14875882609045381828)
XLA Ops:
  0.0 1.9 %shard_map.100 = f32[576,128]{1,0:T(8,128)} custom-call(s32[64]{0:T(128)} %refs_0_.1, s32[64]{0:T(128)} %refs_1_.1, f32[128,128]{1,0:T(8,128)} %bitcast.11, f32[64,128]{1,0:T(8,128)} %refs_3_.1, f32[64,128]{1,0:T(8,128)} %refs_4_.1), custom_call_target="tpu_custom_call" | custom-call | flops 1000000 | bytes 500000 | tf_op jit(solution)/shard_map/pallas_call | solution.py:376
  1.9 0.0 copy-start.2
  1.9 22.1 %all-to-all-start = ((f32[64,1,1152]{2,1,0:T(1,128)}), f32[64,1,1152]{2,1,0:T(1,128)S(1)}, u32[]{:S(2)}, u32[]{:S(2)}) async-start(f32[64,1,1152]{2,1,0:T(1,128)} %bitcast.1), calls=%async_computation | async-start | bytes 589824 | tf_op jit(solution)/shard_map/all_to_all | solution.py:325
  24.1 0.0 copy-start.3
  24.1 13.8 %all-to-all-done = f32[64,1,1152]{2,1,0:T(1,128)S(1)} async-done(((f32[64,1,1152]{2,1,0:T(1,128)}), f32[64,1,1152]{2,1,0:T(1,128)S(1)}, u32[]{:S(2)}, u32[]{:S(2)}) %all-to-all-start) | async-done | bytes 294944 | tf_op jit(solution)/shard_map/all_to_all | solution.py:325
  37.9 0.0 copy-done.2
  37.9 0.0 copy-done.3
  37.9 0.0 copy-start.4
  38.0 0.0 copy-start.1
  38.0 7.0 %shard_map.101 = f32[512,128]{1,0:T(8,128)} custom-call(f32[576,128]{1,0:T(8,128)S(1)} %bitcast.7, f32[64,128]{1,0:T(8,128)S(1)} %copy-done.3, bf16[128,256]{1,0:T(8,128)(2,1)S(1)} %copy-done.2), custom_call_target="tpu_custom_call" | custom-call | flops 1000000000 | bytes 1000000 | tf_op jit(solution)/shard_map/pallas_call | solution.py:398
  45.0 0.0 copy-start
  45.0 9.9 %all-to-all-start.1 = ((f32[32,16,128]{2,1,0:T(8,128)}), f32[32,16,128]{2,1,0:T(8,128)S(1)}, u32[]{:S(2)}, u32[]{:S(2)}) async-start(f32[32,16,128]{2,1,0:T(8,128)} %bitcast.3), calls=%async_computation.1 | async-start | bytes 524288 | tf_op jit(solution)/shard_map/all_to_all | solution.py:325
  54.9 0.0 copy-done.4
  54.9 1.1 %fusion.4 = (f32[512,128]{1,0:T(8,128)S(1)}, f32[512,128]{1,0:T(8,128)S(1)}) fusion(f32[128]{0:T(128)S(1)} %get-tuple-element.7, f32[512]{0:T(512)S(1)} %copy-done.4, f32[128]{0:T(128)S(1)} %get-tuple-element.8), kind=kLoop, calls=%fused_computation.6 | loop fusion | flops 393216 | bytes 527360 | tf_op jit(solution)/shard_map/sin | solution.py:368
  56.0 2.9 %all-to-all-done.1 = f32[32,16,128]{2,1,0:T(8,128)S(1)} async-done(((f32[32,16,128]{2,1,0:T(8,128)}), f32[32,16,128]{2,1,0:T(8,128)S(1)}, u32[]{:S(2)}, u32[]{:S(2)}) %all-to-all-start.1) | async-done | bytes 262176 | tf_op jit(solution)/shard_map/all_to_all | solution.py:325
  58.9 0.0 copy-done.1
  59.0 0.0 copy-done
  59.0 1.2 %shard_map.102 = f32[128,128]{1,0:T(8,128)S(1)} custom-call(f32[512,128]{1,0:T(8,128)S(1)} %bitcast.8, bf16[1024,512]{1,0:T(8,128)(2,1)S(1)} %copy-done.1, bf16[1024,512]{1,0:T(8,128)(2,1)S(1)} %copy-done, f32[512,128]{1,0:T(8,128)S(1)} %get-tuple-element.6.cos_ref, f32[512,128]{1,0:T(8,128)S(1)} %get-tuple-element.5.sin_ref), custom_call_target="tpu_custom_call" | custom-call | flops 1000000000 | bytes 3000000 | tf_op jit(solution)/shard_map/pallas_call | solution.py:418
  60.2 17.3 %all_to_all.15 = f32[64,2,128]{2,1,0:T(2,128)S(1)} all-to-all(f32[64,2,128]{2,1,0:T(2,128)S(1)} %bitcast.10), channel_id=1, replica_groups={{320,328,336,344,352,360,368,376,256,264,272,280,288,296,304,312,448,45..., dimensions={0} | all-to-all | bytes 131072 | tf_op jit(solution)/shard_map/all_to_all | solution.py:325
  77.4 0.7 shard_map.103
  (1 shorter events, 0.0 us)
Async XLA Ops:
  1.9 36.0 %copy-start.2 = (bf16[128,256]{1,0:T(8,128)(2,1)S(1)}, bf16[128,256]{1,0:T(8,128)(2,1)}, u32[]{:S(2)}) copy-start(bf16[128,256]{1,0:T(8,128)(2,1)} %constant.85.clone.last_ref) | copy-start | bytes 196612
  1.9 36.0 %all-to-all-start = ((f32[64,1,1152]{2,1,0:T(1,128)}), f32[64,1,1152]{2,1,0:T(1,128)S(1)}, u32[]{:S(2)}, u32[]{:S(2)}) async-start(f32[64,1,1152]{2,1,0:T(1,128)} %bitcast.1), calls=%async_computation | async-start | bytes 589824 | tf_op jit(solution)/shard_map/all_to_all | solution.py:325
  24.1 13.9 %copy-start.3 = (f32[64,128]{1,0:T(8,128)S(1)}, f32[64,128]{1,0:T(8,128)}, u32[]{:S(2)}) copy-start(f32[64,128]{1,0:T(8,128)} %constant.84.clone.twist_ref) | copy-start | bytes 98308
  37.9 17.0 %copy-start.4 = (f32[512]{0:T(512)S(1)}, f32[512]{0:T(512)}, u32[]{:S(2)}) copy-start(f32[512]{0:T(512)} %constant.95) | copy-start | bytes 6148
  38.0 21.0 %copy-start.1 = (bf16[1024,512]{1,0:T(8,128)(2,1)S(1)}, bf16[1024,512]{1,0:T(8,128)(2,1)}, u32[]{:S(2)}) copy-start(bf16[1024,512]{1,0:T(8,128)(2,1)} %constant.86.clone.upper_ref) | copy-start | bytes 3145732
  45.0 13.9 %copy-start = (bf16[1024,512]{1,0:T(8,128)(2,1)S(1)}, bf16[1024,512]{1,0:T(8,128)(2,1)}, u32[]{:S(2)}) copy-start(bf16[1024,512]{1,0:T(8,128)(2,1)} %constant.87.clone.lower_ref) | copy-start | bytes 3145732
  45.0 13.9 %all-to-all-start.1 = ((f32[32,16,128]{2,1,0:T(8,128)}), f32[32,16,128]{2,1,0:T(8,128)S(1)}, u32[]{:S(2)}, u32[]{:S(2)}) async-start(f32[32,16,128]{2,1,0:T(8,128)} %bitcast.3), calls=%async_computation.1 | async-start | bytes 524288 | tf_op jit(solution)/shard_map/all_to_all | solution.py:325

commit v7 on v5

--- a/solution.py
+++ b/solution.py
@@ -260,16 +260,15 @@
 def sum_kernel(got_ref, out_ref):
     line = lax.broadcasted_iota(jnp.int32, (8, LANES), 0)
     group = lax.broadcasted_iota(jnp.int32, (8, LANES), 1) // SUB
-    straight = (line // 4) == jnp.bitwise_and(line, 1)
+    parts = [got_ref[8 * step : 8 * step + 8, :] for step in range(Z_CHIPS)]
+    while len(parts) > 1:
+        parts = [a + b for a, b in zip(parts[::2], parts[1::2])]
     result = jnp.zeros((8, LANES), f32)
     for place in range(X_CHIPS):
         chip = (place + FIRST_X) % X_CHIPS
-        total = got_ref[pl.ds(place * 2 * Z_CHIPS, 8), :]
-        for step in range(1, 2 * Z_CHIPS // 8):
-            total = total + got_ref[pl.ds(place * 2 * Z_CHIPS + 8 * step, 8), :]
-        total = total + pltpu.roll(total, 4, 0)
-        total = total + pltpu.roll(total, 2, 0)
-        total = jnp.where(straight, total, pltpu.roll(total, 1, 0))
+        total = jnp.where(
+            line < 4, parts[0][2 * place : 2 * place + 1], parts[0][2 * place + 1 : 2 * place + 2]
+        )
         for part in range(X_CHIPS):
             shift = (chip - part) % X_CHIPS
             moved = pltpu.roll(total, SUB * shift, 1) if shift else total
@@ -313,8 +312,13 @@
     return ((i + first_slow) % slow * fast + (j + first_fast) % fast).reshape(-1)
 
 
+def far_members(first_z):
+    z, x = np.meshgrid(np.arange(Z_CHIPS), np.arange(X_CHIPS), indexing="ij")
+    return ((x + FIRST_X) % X_CHIPS * Z_CHIPS + (z + first_z) % Z_CHIPS).reshape(-1)
+
+
 def layer_members():
-    return rotated(X_CHIPS, Z_CHIPS, FIRST_X, TILE_Z)
+    return far_members(TILE_Z)
 
 
 def column_members():
@@ -322,7 +326,7 @@
 
 
 def image_members():
-    return rotated(X_CHIPS, Z_CHIPS, FIRST_X, IMAGE_Z)
+    return far_members(IMAGE_Z)
 
 
 def exchange(value, axes, members):
@@ -363,7 +367,7 @@
         - IMG_M // 2
     )
     place = (lax.axis_index("z") + Z_CHIPS - TILE_Z) % Z_CHIPS
-    layer = ((lane // SUB) * Z_CHIPS + place).astype(f32)
+    layer = (place * X_CHIPS + lane // SUB).astype(f32)
     w_value = w_reach * (2.0 * layer + 1.0 - LAYERS) / LAYERS
     l_direction = lines[:, None] * cell_size
     m_direction = m_index.astype(f32)[None, :] * cell_size

time: 77.9 us -> 78 us (level)
  waiting for transfers between devices: 16.8 us -> 15.7 us
    all_to_all x2, waiting for transfers between devices: 16.8 us -> 15.7 us  [exchange(): lax.all_to_all(value, axes, split_axis=0, concat_axis=0, tiled=True, axis...]
where the time goes in v7:
time: 78 us; the launch traced here: 77.2 us
  starting transfers between devices  32.7 us (42%)
  blocking collectives  17.6 us (23%)
  waiting for transfers between devices  15.7 us (20%)
  Pallas kernels  9.77 us (13%)
  other arithmetic  1.12 us (1%)
    all_to_all x2, starting transfers between devices, exchange(): lax.all_to_all(value, axes, split_axis=0, concat_axis=0, tiled=True, axis...  32.7 us
    all_to_all x1, blocking collectives, exchange(): lax.all_to_all(value, axes, split_axis=0, concat_axis=0, tiled=True, axis...  17.6 us
    all_to_all x2, waiting for transfers between devices, exchange(): lax.all_to_all(value, axes, split_axis=0, concat_axis=0, tiled=True, axis...  15.7 us
    pallas_call x1, Pallas kernels, body(): call(grid_kernel, (PEERS * 2 * PAIRS, LANES), [VMEM] * 3, [pltpu.VMEM((2...  5.97 us
    pallas_call x1, Pallas kernels, body(): call(route_kernel, (LAYERS * SENT, VIS), [HBM] * 5, [pltpu.SMEM((tiles,),...  1.89 us
  transfers between devices with their start and end apart: 2, of which 2 were waited for; matrix products, arithmetic and copies ran while one was open for 1% of the time, Pallas kernels for 0%

profile of v7, /device:TPU:1, one launch (start us, length us, event | category | flops | bytes accessed | tf_op | source)
XLA Modules:
  0.0 77.2 jit_solution(6629490215945105956)
XLA Ops:
  0.0 1.9 %shard_map.100 = f32[576,128]{1,0:T(8,128)} custom-call(s32[64]{0:T(128)} %refs_0_.1, s32[64]{0:T(128)} %refs_1_.1, f32[128,128]{1,0:T(8,128)} %bitcast.12, f32[64,128]{1,0:T(8,128)} %refs_3_.1, f32[64,128]{1,0:T(8,128)} %refs_4_.1), custom_call_target="tpu_custom_call" | custom-call | flops 1000000 | bytes 500000 | tf_op jit(solution)/shard_map/pallas_call | solution.py:385
  1.9 0.0 copy-start.2
  1.9 22.1 %all-to-all-start = ((f32[64,1,1152]{2,1,0:T(1,128)}), f32[64,1,1152]{2,1,0:T(1,128)S(1)}, u32[]{:S(2)}, u32[]{:S(2)}) async-start(f32[64,1,1152]{2,1,0:T(1,128)} %bitcast.11), calls=%async_computation | async-start | bytes 589824 | tf_op jit(solution)/shard_map/all_to_all | solution.py:334
  24.0 0.0 copy-start.3
  24.0 12.8 %all-to-all-done = f32[64,1,1152]{2,1,0:T(1,128)S(1)} async-done(((f32[64,1,1152]{2,1,0:T(1,128)}), f32[64,1,1152]{2,1,0:T(1,128)S(1)}, u32[]{:S(2)}, u32[]{:S(2)}) %all-to-all-start) | async-done | bytes 294944 | tf_op jit(solution)/shard_map/all_to_all | solution.py:334
  36.9 0.0 copy-done.2
  36.9 0.0 copy-done.3
  36.9 0.0 copy-start.4
  36.9 0.0 copy-start.1
  36.9 6.0 %shard_map.101 = f32[512,128]{1,0:T(8,128)} custom-call(f32[576,128]{1,0:T(8,128)S(1)} %bitcast.7, f32[64,128]{1,0:T(8,128)S(1)} %copy-done.3, bf16[128,256]{1,0:T(8,128)(2,1)S(1)} %copy-done.2), custom_call_target="tpu_custom_call" | custom-call | flops 1000000000 | bytes 1000000 | tf_op jit(solution)/shard_map/pallas_call | solution.py:406
  42.9 0.0 copy-start
  42.9 10.7 %all-to-all-start.1 = ((f32[32,16,128]{2,1,0:T(8,128)}), f32[32,16,128]{2,1,0:T(8,128)S(1)}, u32[]{:S(2)}, u32[]{:S(2)}) async-start(f32[32,16,128]{2,1,0:T(8,128)} %bitcast.3), calls=%async_computation.1 | async-start | bytes 524288 | tf_op jit(solution)/shard_map/all_to_all | solution.py:334
  53.6 0.0 copy-done.4
  53.6 1.1 %fusion.4 = (f32[512,128]{1,0:T(8,128)S(1)}, f32[512,128]{1,0:T(8,128)S(1)}) fusion(f32[128]{0:T(128)S(1)} %get-tuple-element.7, f32[512]{0:T(512)S(1)} %copy-done.4, f32[128]{0:T(128)S(1)} %get-tuple-element.8), kind=kLoop, calls=%fused_computation.6 | loop fusion | flops 393216 | bytes 527360 | tf_op jit(solution)/shard_map/sin | solution.py:377
  54.7 2.9 %all-to-all-done.1 = f32[32,16,128]{2,1,0:T(8,128)S(1)} async-done(((f32[32,16,128]{2,1,0:T(8,128)}), f32[32,16,128]{2,1,0:T(8,128)S(1)}, u32[]{:S(2)}, u32[]{:S(2)}) %all-to-all-start.1) | async-done | bytes 262176 | tf_op jit(solution)/shard_map/all_to_all | solution.py:334
  57.6 0.0 copy-done.1
  57.6 0.0 copy-done
  57.6 1.2 %shard_map.102 = f32[128,128]{1,0:T(8,128)S(1)} custom-call(f32[512,128]{1,0:T(8,128)S(1)} %bitcast.8, bf16[1024,512]{1,0:T(8,128)(2,1)S(1)} %copy-done.1, bf16[1024,512]{1,0:T(8,128)(2,1)S(1)} %copy-done, f32[512,128]{1,0:T(8,128)S(1)} %get-tuple-element.6.cos_ref, f32[512,128]{1,0:T(8,128)S(1)} %get-tuple-element.5.sin_ref), custom_call_target="tpu_custom_call" | custom-call | flops 1000000000 | bytes 3000000 | tf_op jit(solution)/shard_map/pallas_call | solution.py:425
  58.8 17.6 %all_to_all.15 = f32[64,2,128]{2,1,0:T(2,128)S(1)} all-to-all(f32[64,2,128]{2,1,0:T(2,128)S(1)} %bitcast.10), channel_id=1, replica_groups={{320,448,64,192,328,456,72,200,336,464,80,208,344,472,88,216,352,480,96..., dimensions={0} | all-to-all | bytes 131072 | tf_op jit(solution)/shard_map/all_to_all | solution.py:334
  76.5 0.7 shard_map.103
  (1 shorter events, 0.0 us)
Async XLA Ops:
  1.9 35.0 %copy-start.2 = (bf16[128,256]{1,0:T(8,128)(2,1)S(1)}, bf16[128,256]{1,0:T(8,128)(2,1)}, u32[]{:S(2)}) copy-start(bf16[128,256]{1,0:T(8,128)(2,1)} %constant.86.clone.last_ref) | copy-start | bytes 196612
  1.9 34.9 %all-to-all-start = ((f32[64,1,1152]{2,1,0:T(1,128)}), f32[64,1,1152]{2,1,0:T(1,128)S(1)}, u32[]{:S(2)}, u32[]{:S(2)}) async-start(f32[64,1,1152]{2,1,0:T(1,128)} %bitcast.11), calls=%async_computation | async-start | bytes 589824 | tf_op jit(solution)/shard_map/all_to_all | solution.py:334
  24.0 12.9 %copy-start.3 = (f32[64,128]{1,0:T(8,128)S(1)}, f32[64,128]{1,0:T(8,128)}, u32[]{:S(2)}) copy-start(f32[64,128]{1,0:T(8,128)} %constant.85.clone.twist_ref) | copy-start | bytes 98308
  36.9 16.7 %copy-start.4 = (f32[512]{0:T(512)S(1)}, f32[512]{0:T(512)}, u32[]{:S(2)}) copy-start(f32[512]{0:T(512)} %constant.96) | copy-start | bytes 6148
  36.9 20.7 %copy-start.1 = (bf16[1024,512]{1,0:T(8,128)(2,1)S(1)}, bf16[1024,512]{1,0:T(8,128)(2,1)}, u32[]{:S(2)}) copy-start(bf16[1024,512]{1,0:T(8,128)(2,1)} %constant.87.clone.upper_ref) | copy-start | bytes 3145732
  42.9 14.8 %copy-start = (bf16[1024,512]{1,0:T(8,128)(2,1)S(1)}, bf16[1024,512]{1,0:T(8,128)(2,1)}, u32[]{:S(2)}) copy-start(bf16[1024,512]{1,0:T(8,128)(2,1)} %constant.88.clone.lower_ref) | copy-start | bytes 3145732
  42.9 14.7 %all-to-all-start.1 = ((f32[32,16,128]{2,1,0:T(8,128)}), f32[32,16,128]{2,1,0:T(8,128)S(1)}, u32[]{:S(2)}, u32[]{:S(2)}) async-start(f32[32,16,128]{2,1,0:T(8,128)} %bitcast.3), calls=%async_computation.1 | async-start | bytes 524288 | tf_op jit(solution)/shard_map/all_to_all | solution.py:334

commit v8 on v5

--- a/solution.py
+++ b/solution.py
@@ -33,6 +33,7 @@
 SENT = 4 * CAP + 1
 PEERS = X_CHIPS * N_SLAB
 PAIRS = RB // 2
+EARLY = 8
 NARROW = math.sqrt(0.5 / math.log(2.0))
 
 
@@ -127,7 +128,17 @@
 
 
 def grid_kernel(
-    got_ref, twist_ref, last_ref, out_ref, grid_ref, upper_ref, lower_ref, name_ref, block_ref, sem
+    got_ref,
+    twist_ref,
+    last_ref,
+    out_ref,
+    grid_ref,
+    upper_ref,
+    lower_ref,
+    early_ref,
+    name_ref,
+    block_ref,
+    sem,
 ):
     named = got_ref[pl.ds(4 * CAP, LAYERS, stride=SENT), :]
     source = lax.broadcasted_iota(jnp.int32, (LAYERS, SLOTS), 0)
@@ -143,9 +154,8 @@
     ).T * NARROW
     rows = (lax.broadcasted_iota(jnp.int32, (RB, VIS), 0).astype(f32) + 0.5) * NARROW
     cols = (lax.broadcasted_iota(jnp.int32, (VIS, CB), 1).astype(f32) + 0.5) * NARROW
-    copy.wait()
-
-    def one(source, slot, center):
+
+    def patch(source, slot, center):
         start = source * SENT + 4 * slot
         real = got_ref[pl.ds(start, 1), :]
         imag = got_ref[pl.ds(start + 1, 1), :]
@@ -156,19 +166,30 @@
         col_upper, col_lower = split(jnp.exp2(-(away * away)))
         left = jnp.concatenate([upper, lower], 0)
         both = dot(left, jnp.concatenate([col_upper, col_lower], 1), NN)
-        patch = both[:, :CB] + both[:, CB:]
-        grid_ref[block_ref[0, slot * LAYERS + source]] += patch[: 2 * RB] + patch[2 * RB :]
-
-    together = 16
+        half = both[:, :CB] + both[:, CB:]
+        return half[: 2 * RB] + half[2 * RB :]
+
+    early = [(source, slot) for source in range(EARLY) for slot in range(CAP)]
+    for index, (source, slot) in enumerate(early):
+        lane = slot * LAYERS + source
+        early_ref[index] = patch(source, slot, offsets[:, lane : lane + 1])
+    copy.wait()
+    for index, (source, slot) in enumerate(early):
+        grid_ref[block_ref[0, slot * LAYERS + source]] += early_ref[index]
+
+    together = (LAYERS - EARLY) // 2
 
     def some(step, held):
         for part in range(together):
             for slot in range(CAP):
+                source = EARLY + step * together + part
                 lane = slot * LAYERS + part
-                one(step * together + part, slot, held[:, lane : lane + 1])
+                grid_ref[block_ref[0, slot * LAYERS + source]] += patch(
+                    source, slot, held[:, lane : lane + 1]
+                )
         return pltpu.roll(held, SLOTS - together, 1)
 
-    lax.fori_loop(0, LAYERS // together, some, offsets)
+    lax.fori_loop(0, 2, some, pltpu.roll(offsets, SLOTS - EARLY, 1))
 
     wide, narrow = 8, SUB // 8
     for second in range(2):
@@ -314,7 +335,8 @@
 
 
 def layer_members():
-    return rotated(X_CHIPS, Z_CHIPS, FIRST_X, TILE_Z)
+    z, x = np.meshgrid(np.arange(Z_CHIPS), np.arange(X_CHIPS), indexing="ij")
+    return ((x + FIRST_X) % X_CHIPS * Z_CHIPS + (z + TILE_Z) % Z_CHIPS).reshape(-1)
 
 
 def column_members():
@@ -363,7 +385,7 @@
         - IMG_M // 2
     )
     place = (lax.axis_index("z") + Z_CHIPS - TILE_Z) % Z_CHIPS
-    layer = ((lane // SUB) * Z_CHIPS + place).astype(f32)
+    layer = (place * X_CHIPS + lane // SUB).astype(f32)
     w_value = w_reach * (2.0 * layer + 1.0 - LAYERS) / LAYERS
     l_direction = lines[:, None] * cell_size
     m_direction = m_index.astype(f32)[None, :] * cell_size
@@ -407,6 +429,7 @@
             pltpu.VMEM((2 * SUB, 2 * RB, CB), f32),
             pltpu.VMEM((2 * SUB * RB, 2 * CB), bf16),
             pltpu.VMEM((2 * SUB * RB, 2 * CB), bf16),
+            pltpu.VMEM((EARLY * CAP, 2 * RB, CB), f32),
             pltpu.VMEM((1, SLOTS), jnp.int32),
             pltpu.SMEM((1, SLOTS), jnp.int32),
             pltpu.SemaphoreType.DMA,

time: 77.9 us -> 78 us (level)
  waiting for transfers between devices: 16.8 us -> 15.7 us
  starting transfers between devices: 32 us -> 32.8 us
    all_to_all x2, waiting for transfers between devices: 16.8 us -> 15.7 us  [exchange(): lax.all_to_all(value, axes, split_axis=0, concat_axis=0, tiled=True, axis...]
where the time goes in v8:
time: 78 us; the launch traced here: 77 us
  starting transfers between devices  32.8 us (42%)
  blocking collectives  17.6 us (23%)
  waiting for transfers between devices  15.7 us (20%)
  Pallas kernels  9.67 us (12%)
  other arithmetic  1.12 us (1%)
    all_to_all x2, starting transfers between devices, exchange(): lax.all_to_all(value, axes, split_axis=0, concat_axis=0, tiled=True, axis...  32.8 us
    all_to_all x1, blocking collectives, exchange(): lax.all_to_all(value, axes, split_axis=0, concat_axis=0, tiled=True, axis...  17.6 us
    all_to_all x2, waiting for transfers between devices, exchange(): lax.all_to_all(value, axes, split_axis=0, concat_axis=0, tiled=True, axis...  15.7 us
    pallas_call x1, Pallas kernels, body(): call(grid_kernel, (PEERS * 2 * PAIRS, LANES), [VMEM] * 3, [pltpu.VMEM((2...  5.87 us
    pallas_call x1, Pallas kernels, body(): call(route_kernel, (LAYERS * SENT, VIS), [HBM] * 5, [pltpu.SMEM((tiles,),...  1.89 us
  transfers between devices with their start and end apart: 2, of which 2 were waited for; matrix products, arithmetic and copies ran while one was open for 1% of the time, Pallas kernels for 0%

profile of v8, /device:TPU:1, one launch (start us, length us, event | category | flops | bytes accessed | tf_op | source)
XLA Modules:
  0.0 77.0 jit_solution(2990347620826690409)
XLA Ops:
  0.0 1.9 %shard_map.100 = f32[576,128]{1,0:T(8,128)} custom-call(s32[64]{0:T(128)} %refs_0_.1, s32[64]{0:T(128)} %refs_1_.1, f32[128,128]{1,0:T(8,128)} %bitcast.12, f32[64,128]{1,0:T(8,128)} %refs_3_.1, f32[64,128]{1,0:T(8,128)} %refs_4_.1), custom_call_target="tpu_custom_call" | custom-call | flops 1000000 | bytes 500000 | tf_op jit(solution)/shard_map/pallas_call | solution.py:403
  1.9 0.0 copy-start.2
  1.9 22.1 %all-to-all-start = ((f32[64,1,1152]{2,1,0:T(1,128)}), f32[64,1,1152]{2,1,0:T(1,128)S(1)}, u32[]{:S(2)}, u32[]{:S(2)}) async-start(f32[64,1,1152]{2,1,0:T(1,128)} %bitcast.11), calls=%async_computation | async-start | bytes 589824 | tf_op jit(solution)/shard_map/all_to_all | solution.py:352
  24.0 0.0 copy-start.3
  24.0 12.8 %all-to-all-done = f32[64,1,1152]{2,1,0:T(1,128)S(1)} async-done(((f32[64,1,1152]{2,1,0:T(1,128)}), f32[64,1,1152]{2,1,0:T(1,128)S(1)}, u32[]{:S(2)}, u32[]{:S(2)}) %all-to-all-start) | async-done | bytes 294944 | tf_op jit(solution)/shard_map/all_to_all | solution.py:352
  36.9 0.0 copy-done.2
  36.9 0.0 copy-done.3
  36.9 0.0 copy-start.4
  36.9 0.0 copy-start.1
  36.9 5.9 %shard_map.101 = f32[512,128]{1,0:T(8,128)} custom-call(f32[576,128]{1,0:T(8,128)S(1)} %bitcast.7, f32[64,128]{1,0:T(8,128)S(1)} %copy-done.3, bf16[128,256]{1,0:T(8,128)(2,1)S(1)} %copy-done.2), custom_call_target="tpu_custom_call" | custom-call | flops 1000000000 | bytes 1000000 | tf_op jit(solution)/shard_map/pallas_call | solution.py:424
  42.7 0.0 copy-start
  42.8 10.7 %all-to-all-start.1 = ((f32[32,16,128]{2,1,0:T(8,128)}), f32[32,16,128]{2,1,0:T(8,128)S(1)}, u32[]{:S(2)}, u32[]{:S(2)}) async-start(f32[32,16,128]{2,1,0:T(8,128)} %bitcast.3), calls=%async_computation.1 | async-start | bytes 524288 | tf_op jit(solution)/shard_map/all_to_all | solution.py:352
  53.5 0.0 copy-done.4
  53.5 1.1 %fusion.4 = (f32[512,128]{1,0:T(8,128)S(1)}, f32[512,128]{1,0:T(8,128)S(1)}) fusion(f32[128]{0:T(128)S(1)} %get-tuple-element.7, f32[512]{0:T(512)S(1)} %copy-done.4, f32[128]{0:T(128)S(1)} %get-tuple-element.8), kind=kLoop, calls=%fused_computation.6 | loop fusion | flops 393216 | bytes 527360 | tf_op jit(solution)/shard_map/sin | solution.py:395
  54.6 2.9 %all-to-all-done.1 = f32[32,16,128]{2,1,0:T(8,128)S(1)} async-done(((f32[32,16,128]{2,1,0:T(8,128)}), f32[32,16,128]{2,1,0:T(8,128)S(1)}, u32[]{:S(2)}, u32[]{:S(2)}) %all-to-all-start.1) | async-done | bytes 262176 | tf_op jit(solution)/shard_map/all_to_all | solution.py:352
  57.5 0.0 copy-done.1
  57.5 0.0 copy-done
  57.5 1.2 %shard_map.102 = f32[128,128]{1,0:T(8,128)S(1)} custom-call(f32[512,128]{1,0:T(8,128)S(1)} %bitcast.8, bf16[1024,512]{1,0:T(8,128)(2,1)S(1)} %copy-done.1, bf16[1024,512]{1,0:T(8,128)(2,1)S(1)} %copy-done, f32[512,128]{1,0:T(8,128)S(1)} %get-tuple-element.6.cos_ref, f32[512,128]{1,0:T(8,128)S(1)} %get-tuple-element.5.sin_ref), custom_call_target="tpu_custom_call" | custom-call | flops 1000000000 | bytes 3000000 | tf_op jit(solution)/shard_map/pallas_call | solution.py:444
  58.7 17.6 %all_to_all.15 = f32[64,2,128]{2,1,0:T(2,128)S(1)} all-to-all(f32[64,2,128]{2,1,0:T(2,128)S(1)} %bitcast.10), channel_id=1, replica_groups={{320,328,336,344,352,360,368,376,256,264,272,280,288,296,304,312,448,45..., dimensions={0} | all-to-all | bytes 131072 | tf_op jit(solution)/shard_map/all_to_all | solution.py:352
  76.3 0.7 shard_map.103
  (1 shorter events, 0.0 us)
Async XLA Ops:
  1.9 35.0 %copy-start.2 = (bf16[128,256]{1,0:T(8,128)(2,1)S(1)}, bf16[128,256]{1,0:T(8,128)(2,1)}, u32[]{:S(2)}) copy-start(bf16[128,256]{1,0:T(8,128)(2,1)} %constant.86.clone.last_ref) | copy-start | bytes 196612
  1.9 34.9 %all-to-all-start = ((f32[64,1,1152]{2,1,0:T(1,128)}), f32[64,1,1152]{2,1,0:T(1,128)S(1)}, u32[]{:S(2)}, u32[]{:S(2)}) async-start(f32[64,1,1152]{2,1,0:T(1,128)} %bitcast.11), calls=%async_computation | async-start | bytes 589824 | tf_op jit(solution)/shard_map/all_to_all | solution.py:352
  24.0 12.9 %copy-start.3 = (f32[64,128]{1,0:T(8,128)S(1)}, f32[64,128]{1,0:T(8,128)}, u32[]{:S(2)}) copy-start(f32[64,128]{1,0:T(8,128)} %constant.85.clone.twist_ref) | copy-start | bytes 98308
  36.9 16.6 %copy-start.4 = (f32[512]{0:T(512)S(1)}, f32[512]{0:T(512)}, u32[]{:S(2)}) copy-start(f32[512]{0:T(512)} %constant.96) | copy-start | bytes 6148
  36.9 20.6 %copy-start.1 = (bf16[1024,512]{1,0:T(8,128)(2,1)S(1)}, bf16[1024,512]{1,0:T(8,128)(2,1)}, u32[]{:S(2)}) copy-start(bf16[1024,512]{1,0:T(8,128)(2,1)} %constant.87.clone.upper_ref) | copy-start | bytes 3145732
  42.7 14.8 %copy-start = (bf16[1024,512]{1,0:T(8,128)(2,1)S(1)}, bf16[1024,512]{1,0:T(8,128)(2,1)}, u32[]{:S(2)}) copy-start(bf16[1024,512]{1,0:T(8,128)(2,1)} %constant.88.clone.lower_ref) | copy-start | bytes 3145732
  42.8 14.8 %all-to-all-start.1 = ((f32[32,16,128]{2,1,0:T(8,128)}), f32[32,16,128]{2,1,0:T(8,128)S(1)}, u32[]{:S(2)}, u32[]{:S(2)}) async-start(f32[32,16,128]{2,1,0:T(8,128)} %bitcast.3), calls=%async_computation.1 | async-start | bytes 524288 | tf_op jit(solution)/shard_map/all_to_all | solution.py:352

commit v9 on v8

--- a/solution.py
+++ b/solution.py
@@ -25,7 +25,7 @@
 Z_CHIPS = 16
 FIRST_X = 2
 FIRST_SLAB = 4
-TILE_Z = 9
+TILE_Z = 11
 IMAGE_Z = 8
 SUB = 32
 SLOTS = LAYERS * CAP

time: 78 us -> 77.7 us (level)
  starting transfers between devices: 32.8 us -> 31.1 us
  waiting for transfers between devices: 15.7 us -> 17.2 us
    all_to_all x2, starting transfers between devices: 32.8 us -> 31.1 us  [exchange(): lax.all_to_all(value, axes, split_axis=0, concat_axis=0, tiled=True, axis...]
    all_to_all x2, waiting for transfers between devices: 15.7 us -> 17.2 us  [exchange(): lax.all_to_all(value, axes, split_axis=0, concat_axis=0, tiled=True, axis...]
where the time goes in v9:
time: 77.7 us; the launch traced here: 76.7 us
  starting transfers between devices  31.1 us (40%)
  blocking collectives  17.5 us (23%)
  waiting for transfers between devices  17.2 us (22%)
  Pallas kernels  9.67 us (12%)
  other arithmetic  1.12 us (1%)
    all_to_all x2, starting transfers between devices, exchange(): lax.all_to_all(value, axes, split_axis=0, concat_axis=0, tiled=True, axis...  31.1 us
    all_to_all x1, blocking collectives, exchange(): lax.all_to_all(value, axes, split_axis=0, concat_axis=0, tiled=True, axis...  17.5 us
    all_to_all x2, waiting for transfers between devices, exchange(): lax.all_to_all(value, axes, split_axis=0, concat_axis=0, tiled=True, axis...  17.2 us
    pallas_call x1, Pallas kernels, body(): call(grid_kernel, (PEERS * 2 * PAIRS, LANES), [VMEM] * 3, [pltpu.VMEM((2...  5.87 us
    pallas_call x1, Pallas kernels, body(): call(route_kernel, (LAYERS * SENT, VIS), [HBM] * 5, [pltpu.SMEM((tiles,),...  1.89 us
  transfers between devices with their start and end apart: 2, of which 2 were waited for; matrix products, arithmetic and copies ran while one was open for 1% of the time, Pallas kernels for 0%

profile of v9, /device:TPU:1, one launch (start us, length us, event | category | flops | bytes accessed | tf_op | source)
XLA Modules:
  0.0 76.7 jit_solution(11171266786188058248)
XLA Ops:
  0.0 1.9 %shard_map.100 = f32[576,128]{1,0:T(8,128)} custom-call(s32[64]{0:T(128)} %refs_0_.1, s32[64]{0:T(128)} %refs_1_.1, f32[128,128]{1,0:T(8,128)} %bitcast.12, f32[64,128]{1,0:T(8,128)} %refs_3_.1, f32[64,128]{1,0:T(8,128)} %refs_4_.1), custom_call_target="tpu_custom_call" | custom-call | flops 1000000 | bytes 500000 | tf_op jit(solution)/shard_map/pallas_call | solution.py:403
  1.9 0.0 copy-start.2
  1.9 20.2 %all-to-all-start = ((f32[64,1,1152]{2,1,0:T(1,128)}), f32[64,1,1152]{2,1,0:T(1,128)S(1)}, u32[]{:S(2)}, u32[]{:S(2)}) async-start(f32[64,1,1152]{2,1,0:T(1,128)} %bitcast.11), calls=%async_computation | async-start | bytes 589824 | tf_op jit(solution)/shard_map/all_to_all | solution.py:352
  22.2 0.0 copy-start.3
  22.2 14.3 %all-to-all-done = f32[64,1,1152]{2,1,0:T(1,128)S(1)} async-done(((f32[64,1,1152]{2,1,0:T(1,128)}), f32[64,1,1152]{2,1,0:T(1,128)S(1)}, u32[]{:S(2)}, u32[]{:S(2)}) %all-to-all-start) | async-done | bytes 294944 | tf_op jit(solution)/shard_map/all_to_all | solution.py:352
  36.5 0.0 copy-done.2
  36.5 0.0 copy-done.3
  36.5 0.0 copy-start.4
  36.5 0.0 copy-start.1
  36.5 5.9 %shard_map.101 = f32[512,128]{1,0:T(8,128)} custom-call(f32[576,128]{1,0:T(8,128)S(1)} %bitcast.7, f32[64,128]{1,0:T(8,128)S(1)} %copy-done.3, bf16[128,256]{1,0:T(8,128)(2,1)S(1)} %copy-done.2), custom_call_target="tpu_custom_call" | custom-call | flops 1000000000 | bytes 1000000 | tf_op jit(solution)/shard_map/pallas_call | solution.py:424
  42.4 0.0 copy-start
  42.4 10.9 %all-to-all-start.1 = ((f32[32,16,128]{2,1,0:T(8,128)}), f32[32,16,128]{2,1,0:T(8,128)S(1)}, u32[]{:S(2)}, u32[]{:S(2)}) async-start(f32[32,16,128]{2,1,0:T(8,128)} %bitcast.3), calls=%async_computation.1 | async-start | bytes 524288 | tf_op jit(solution)/shard_map/all_to_all | solution.py:352
  53.3 0.0 copy-done.4
  53.3 1.1 %fusion.4 = (f32[512,128]{1,0:T(8,128)S(1)}, f32[512,128]{1,0:T(8,128)S(1)}) fusion(f32[128]{0:T(128)S(1)} %get-tuple-element.7, f32[512]{0:T(512)S(1)} %copy-done.4, f32[128]{0:T(128)S(1)} %get-tuple-element.8), kind=kLoop, calls=%fused_computation.6 | loop fusion | flops 393216 | bytes 527360 | tf_op jit(solution)/shard_map/sin | solution.py:395
  54.4 2.9 %all-to-all-done.1 = f32[32,16,128]{2,1,0:T(8,128)S(1)} async-done(((f32[32,16,128]{2,1,0:T(8,128)}), f32[32,16,128]{2,1,0:T(8,128)S(1)}, u32[]{:S(2)}, u32[]{:S(2)}) %all-to-all-start.1) | async-done | bytes 262176 | tf_op jit(solution)/shard_map/all_to_all | solution.py:352
  57.3 0.0 copy-done.1
  57.3 0.0 copy-done
  57.3 1.2 %shard_map.102 = f32[128,128]{1,0:T(8,128)S(1)} custom-call(f32[512,128]{1,0:T(8,128)S(1)} %bitcast.8, bf16[1024,512]{1,0:T(8,128)(2,1)S(1)} %copy-done.1, bf16[1024,512]{1,0:T(8,128)(2,1)S(1)} %copy-done, f32[512,128]{1,0:T(8,128)S(1)} %get-tuple-element.6.cos_ref, f32[512,128]{1,0:T(8,128)S(1)} %get-tuple-element.5.sin_ref), custom_call_target="tpu_custom_call" | custom-call | flops 1000000000 | bytes 3000000 | tf_op jit(solution)/shard_map/pallas_call | solution.py:444
  58.6 17.5 %all_to_all.15 = f32[64,2,128]{2,1,0:T(2,128)S(1)} all-to-all(f32[64,2,128]{2,1,0:T(2,128)S(1)} %bitcast.10), channel_id=1, replica_groups={{320,328,336,344,352,360,368,376,256,264,272,280,288,296,304,312,448,45..., dimensions={0} | all-to-all | bytes 131072 | tf_op jit(solution)/shard_map/all_to_all | solution.py:352
  76.0 0.7 shard_map.103
  (1 shorter events, 0.0 us)
Async XLA Ops:
  1.9 34.6 %copy-start.2 = (bf16[128,256]{1,0:T(8,128)(2,1)S(1)}, bf16[128,256]{1,0:T(8,128)(2,1)}, u32[]{:S(2)}) copy-start(bf16[128,256]{1,0:T(8,128)(2,1)} %constant.85.clone.last_ref) | copy-start | bytes 196612
  1.9 34.6 %all-to-all-start = ((f32[64,1,1152]{2,1,0:T(1,128)}), f32[64,1,1152]{2,1,0:T(1,128)S(1)}, u32[]{:S(2)}, u32[]{:S(2)}) async-start(f32[64,1,1152]{2,1,0:T(1,128)} %bitcast.11), calls=%async_computation | async-start | bytes 589824 | tf_op jit(solution)/shard_map/all_to_all | solution.py:352
  22.2 14.3 %copy-start.3 = (f32[64,128]{1,0:T(8,128)S(1)}, f32[64,128]{1,0:T(8,128)}, u32[]{:S(2)}) copy-start(f32[64,128]{1,0:T(8,128)} %constant.84.clone.twist_ref) | copy-start | bytes 98308
  36.5 16.8 %copy-start.4 = (f32[512]{0:T(512)S(1)}, f32[512]{0:T(512)}, u32[]{:S(2)}) copy-start(f32[512]{0:T(512)} %constant.95) | copy-start | bytes 6148
  36.5 20.8 %copy-start.1 = (bf16[1024,512]{1,0:T(8,128)(2,1)S(1)}, bf16[1024,512]{1,0:T(8,128)(2,1)}, u32[]{:S(2)}) copy-start(bf16[1024,512]{1,0:T(8,128)(2,1)} %constant.86.clone.upper_ref) | copy-start | bytes 3145732
  42.4 15.0 %copy-start = (bf16[1024,512]{1,0:T(8,128)(2,1)S(1)}, bf16[1024,512]{1,0:T(8,128)(2,1)}, u32[]{:S(2)}) copy-start(bf16[1024,512]{1,0:T(8,128)(2,1)} %constant.87.clone.lower_ref) | copy-start | bytes 3145732
  42.4 14.9 %all-to-all-start.1 = ((f32[32,16,128]{2,1,0:T(8,128)}), f32[32,16,128]{2,1,0:T(8,128)S(1)}, u32[]{:S(2)}, u32[]{:S(2)}) async-start(f32[32,16,128]{2,1,0:T(8,128)} %bitcast.3), calls=%async_computation.1 | async-start | bytes 524288 | tf_op jit(solution)/shard_map/all_to_all | solution.py:352

commit v10 on v8

--- a/solution.py
+++ b/solution.py
@@ -253,9 +253,11 @@
                 for y in range(2):
                     for h in range(2):
                         step = 2 * (h * blocks + high) + y
-                        row = layer * N_SLAB * 2 * PAIRS + step
+                        row = layer * 2 * PAIRS + step
                         parts.append(
-                            swap_blocks(got_ref[pl.ds(row, N_SLAB, stride=2 * PAIRS), :])
+                            swap_blocks(
+                                got_ref[pl.ds(row, N_SLAB, stride=X_CHIPS * 2 * PAIRS), :]
+                            )
                         )
                 lines.append(jnp.concatenate(parts, 1))
             upper, lower = split(jnp.concatenate(lines, 0))
@@ -340,7 +342,8 @@
 
 
 def column_members():
-    return rotated(X_CHIPS, N_SLAB, FIRST_X, FIRST_SLAB)
+    slab, x = np.meshgrid(np.arange(N_SLAB), np.arange(X_CHIPS), indexing="ij")
+    return ((x + FIRST_X) % X_CHIPS * N_SLAB + (slab + FIRST_SLAB) % N_SLAB).reshape(-1)
 
 
 def image_members():

time: 78 us -> 78.6 us (level)
  blocking collectives: 17.6 us -> 18.9 us
    all_to_all x1, blocking collectives: 17.6 us -> 18.9 us  [exchange(): lax.all_to_all(value, axes, split_axis=0, concat_axis=0, tiled=True, axis...]
where the time goes in v10:
time: 78.6 us; the launch traced here: 78.3 us
  starting transfers between devices  32.7 us (42%)
  blocking collectives  18.9 us (24%)
  waiting for transfers between devices  15.7 us (20%)
  Pallas kernels  9.76 us (12%)
  other arithmetic  1.12 us (1%)
    all_to_all x2, starting transfers between devices, exchange(): lax.all_to_all(value, axes, split_axis=0, concat_axis=0, tiled=True, axis...  32.7 us
    all_to_all x1, blocking collectives, exchange(): lax.all_to_all(value, axes, split_axis=0, concat_axis=0, tiled=True, axis...  18.9 us
    all_to_all x2, waiting for transfers between devices, exchange(): lax.all_to_all(value, axes, split_axis=0, concat_axis=0, tiled=True, axis...  15.7 us
    pallas_call x1, Pallas kernels, body(): call(grid_kernel, (PEERS * 2 * PAIRS, LANES), [VMEM] * 3, [pltpu.VMEM((2...  5.95 us
    pallas_call x1, Pallas kernels, body(): call(route_kernel, (LAYERS * SENT, VIS), [HBM] * 5, [pltpu.SMEM((tiles,),...  1.89 us
  transfers between devices with their start and end apart: 2, of which 2 were waited for; matrix products, arithmetic and copies ran while one was open for 1% of the time, Pallas kernels for 0%

profile of v10, /device:TPU:1, one launch (start us, length us, event | category | flops | bytes accessed | tf_op | source)
XLA Modules:
  0.0 78.3 jit_solution(3175823092851053860)
XLA Ops:
  0.0 1.9 %shard_map.100 = f32[576,128]{1,0:T(8,128)} custom-call(s32[64]{0:T(128)} %refs_0_.1, s32[64]{0:T(128)} %refs_1_.1, f32[128,128]{1,0:T(8,128)} %bitcast.12, f32[64,128]{1,0:T(8,128)} %refs_3_.1, f32[64,128]{1,0:T(8,128)} %refs_4_.1), custom_call_target="tpu_custom_call" | custom-call | flops 1000000 | bytes 500000 | tf_op jit(solution)/shard_map/pallas_call | solution.py:406
  1.9 0.0 copy-start.2
  1.9 22.1 %all-to-all-start = ((f32[64,1,1152]{2,1,0:T(1,128)}), f32[64,1,1152]{2,1,0:T(1,128)S(1)}, u32[]{:S(2)}, u32[]{:S(2)}) async-start(f32[64,1,1152]{2,1,0:T(1,128)} %bitcast.11), calls=%async_computation | async-start | bytes 589824 | tf_op jit(solution)/shard_map/all_to_all | solution.py:355
  24.0 0.0 copy-start.3
  24.0 12.8 %all-to-all-done = f32[64,1,1152]{2,1,0:T(1,128)S(1)} async-done(((f32[64,1,1152]{2,1,0:T(1,128)}), f32[64,1,1152]{2,1,0:T(1,128)S(1)}, u32[]{:S(2)}, u32[]{:S(2)}) %all-to-all-start) | async-done | bytes 294944 | tf_op jit(solution)/shard_map/all_to_all | solution.py:355
  36.9 0.0 copy-done.2
  36.9 0.0 copy-done.3
  36.9 0.0 copy-start.4
  36.9 0.0 copy-start.1
  36.9 6.0 %shard_map.101 = f32[512,128]{1,0:T(8,128)} custom-call(f32[576,128]{1,0:T(8,128)S(1)} %bitcast.7, f32[64,128]{1,0:T(8,128)S(1)} %copy-done.3, bf16[128,256]{1,0:T(8,128)(2,1)S(1)} %copy-done.2), custom_call_target="tpu_custom_call" | custom-call | flops 1000000000 | bytes 1000000 | tf_op jit(solution)/shard_map/pallas_call | solution.py:427
  42.8 0.0 copy-start
  42.8 10.6 %all-to-all-start.1 = ((f32[32,16,128]{2,1,0:T(8,128)}), f32[32,16,128]{2,1,0:T(8,128)S(1)}, u32[]{:S(2)}, u32[]{:S(2)}) async-start(f32[32,16,128]{2,1,0:T(8,128)} %bitcast.3), calls=%async_computation.1 | async-start | bytes 524288 | tf_op jit(solution)/shard_map/all_to_all | solution.py:355
  53.5 0.0 copy-done.4
  53.5 1.1 %fusion.4 = (f32[512,128]{1,0:T(8,128)S(1)}, f32[512,128]{1,0:T(8,128)S(1)}) fusion(f32[128]{0:T(128)S(1)} %get-tuple-element.7, f32[512]{0:T(512)S(1)} %copy-done.4, f32[128]{0:T(128)S(1)} %get-tuple-element.8), kind=kLoop, calls=%fused_computation.6 | loop fusion | flops 393216 | bytes 527360 | tf_op jit(solution)/shard_map/sin | solution.py:398
  54.6 2.9 %all-to-all-done.1 = f32[32,16,128]{2,1,0:T(8,128)S(1)} async-done(((f32[32,16,128]{2,1,0:T(8,128)}), f32[32,16,128]{2,1,0:T(8,128)S(1)}, u32[]{:S(2)}, u32[]{:S(2)}) %all-to-all-start.1) | async-done | bytes 262176 | tf_op jit(solution)/shard_map/all_to_all | solution.py:355
  57.5 0.0 copy-done.1
  57.5 0.0 copy-done
  57.5 1.2 %shard_map.102 = f32[128,128]{1,0:T(8,128)S(1)} custom-call(f32[512,128]{1,0:T(8,128)S(1)} %bitcast.8, bf16[1024,512]{1,0:T(8,128)(2,1)S(1)} %copy-done.1, bf16[1024,512]{1,0:T(8,128)(2,1)S(1)} %copy-done, f32[512,128]{1,0:T(8,128)S(1)} %get-tuple-element.6.cos_ref, f32[512,128]{1,0:T(8,128)S(1)} %get-tuple-element.5.sin_ref), custom_call_target="tpu_custom_call" | custom-call | flops 1000000000 | bytes 3000000 | tf_op jit(solution)/shard_map/pallas_call | solution.py:447
  58.7 18.9 %all_to_all.15 = f32[64,2,128]{2,1,0:T(2,128)S(1)} all-to-all(f32[64,2,128]{2,1,0:T(2,128)S(1)} %bitcast.10), channel_id=1, replica_groups={{320,328,336,344,352,360,368,376,256,264,272,280,288,296,304,312,448,45..., dimensions={0} | all-to-all | bytes 131072 | tf_op jit(solution)/shard_map/all_to_all | solution.py:355
  77.6 0.7 shard_map.103
  (1 shorter events, 0.0 us)
Async XLA Ops:
  1.9 35.0 %copy-start.2 = (bf16[128,256]{1,0:T(8,128)(2,1)S(1)}, bf16[128,256]{1,0:T(8,128)(2,1)}, u32[]{:S(2)}) copy-start(bf16[128,256]{1,0:T(8,128)(2,1)} %constant.86.clone.last_ref) | copy-start | bytes 196612
  1.9 34.9 %all-to-all-start = ((f32[64,1,1152]{2,1,0:T(1,128)}), f32[64,1,1152]{2,1,0:T(1,128)S(1)}, u32[]{:S(2)}, u32[]{:S(2)}) async-start(f32[64,1,1152]{2,1,0:T(1,128)} %bitcast.11), calls=%async_computation | async-start | bytes 589824 | tf_op jit(solution)/shard_map/all_to_all | solution.py:355
  24.0 12.9 %copy-start.3 = (f32[64,128]{1,0:T(8,128)S(1)}, f32[64,128]{1,0:T(8,128)}, u32[]{:S(2)}) copy-start(f32[64,128]{1,0:T(8,128)} %constant.85.clone.twist_ref) | copy-start | bytes 98308
  36.9 16.6 %copy-start.4 = (f32[512]{0:T(512)S(1)}, f32[512]{0:T(512)}, u32[]{:S(2)}) copy-start(f32[512]{0:T(512)} %constant.96) | copy-start | bytes 6148
  36.9 20.6 %copy-start.1 = (bf16[1024,512]{1,0:T(8,128)(2,1)S(1)}, bf16[1024,512]{1,0:T(8,128)(2,1)}, u32[]{:S(2)}) copy-start(bf16[1024,512]{1,0:T(8,128)(2,1)} %constant.87.clone.upper_ref) | copy-start | bytes 3145732
  42.8 14.7 %copy-start = (bf16[1024,512]{1,0:T(8,128)(2,1)S(1)}, bf16[1024,512]{1,0:T(8,128)(2,1)}, u32[]{:S(2)}) copy-start(bf16[1024,512]{1,0:T(8,128)(2,1)} %constant.88.clone.lower_ref) | copy-start | bytes 3145732
  42.8 14.6 %all-to-all-start.1 = ((f32[32,16,128]{2,1,0:T(8,128)}), f32[32,16,128]{2,1,0:T(8,128)S(1)}, u32[]{:S(2)}, u32[]{:S(2)}) async-start(f32[32,16,128]{2,1,0:T(8,128)} %bitcast.3), calls=%async_computation.1 | async-start | bytes 524288 | tf_op jit(solution)/shard_map/all_to_all | solution.py:355

commit v11 on v8

--- a/solution.py
+++ b/solution.py
@@ -95,8 +95,8 @@
         count_ref[layer] = slot + 1
         start = layer * SENT + slot * 4
         out_ref[pl.ds(start, 2), :] = vis_ref[pl.ds(2 * tile, 2), :]
-        out_ref[pl.ds(start + 2, 1), :] = row_ref[pl.ds(tile, 1), :]
-        out_ref[pl.ds(start + 3, 1), :] = col_ref[pl.ds(tile, 1), :]
+        out_ref[pl.ds(start + 2, 1), :] = row_ref[pl.ds(tile, 1), :] * NARROW
+        out_ref[pl.ds(start + 3, 1), :] = col_ref[pl.ds(tile, 1), :] * NARROW
         named = out_ref.at[pl.ds(layer * SENT + 4 * CAP, 1), :]
         block = jnp.full((1, LANES), block_ref[tile], jnp.int32).astype(f32)
         pltpu.store(named, block, mask=part == slot)
@@ -151,7 +151,7 @@
     grid_ref[...] = jnp.zeros_like(grid_ref)
     offsets = jnp.concatenate(
         [got_ref[pl.ds(4 * slot + 3, LAYERS, stride=SENT), :] for slot in range(CAP)], 0
-    ).T * NARROW
+    ).T
     rows = (lax.broadcasted_iota(jnp.int32, (RB, VIS), 0).astype(f32) + 0.5) * NARROW
     cols = (lax.broadcasted_iota(jnp.int32, (VIS, CB), 1).astype(f32) + 0.5) * NARROW
 
@@ -159,7 +159,7 @@
         start = source * SENT + 4 * slot
         real = got_ref[pl.ds(start, 1), :]
         imag = got_ref[pl.ds(start + 1, 1), :]
-        away = rows - got_ref[pl.ds(start + 2, 1), :] * NARROW
+        away = rows - got_ref[pl.ds(start + 2, 1), :]
         near = jnp.exp2(-(away * away))
         upper, lower = split(jnp.concatenate([near * real, near * imag], 0))
         away = cols - center

time: 78 us -> 78 us (level)
  no operation moved by 1% of the time
where the time goes in v11:
time: 78 us; the launch traced here: 77 us
  starting transfers between devices  32.8 us (42%)
  blocking collectives  17.5 us (22%)
  waiting for transfers between devices  15.7 us (20%)
  Pallas kernels  9.67 us (12%)
  other arithmetic  1.12 us (1%)
    all_to_all x2, starting transfers between devices, exchange(): lax.all_to_all(value, axes, split_axis=0, concat_axis=0, tiled=True, axis...  32.8 us
    all_to_all x1, blocking collectives, exchange(): lax.all_to_all(value, axes, split_axis=0, concat_axis=0, tiled=True, axis...  17.5 us
    all_to_all x2, waiting for transfers between devices, exchange(): lax.all_to_all(value, axes, split_axis=0, concat_axis=0, tiled=True, axis...  15.7 us
    pallas_call x1, Pallas kernels, body(): call(grid_kernel, (PEERS * 2 * PAIRS, LANES), [VMEM] * 3, [pltpu.VMEM((2...  5.88 us
    pallas_call x1, Pallas kernels, body(): call(route_kernel, (LAYERS * SENT, VIS), [HBM] * 5, [pltpu.SMEM((tiles,),...  1.89 us
  transfers between devices with their start and end apart: 2, of which 2 were waited for; matrix products, arithmetic and copies ran while one was open for 1% of the time, Pallas kernels for 0%

profile of v11, /device:TPU:1, one launch (start us, length us, event | category | flops | bytes accessed | tf_op | source)
XLA Modules:
  0.0 77.0 jit_solution(17651432428537840053)
XLA Ops:
  0.0 1.9 %shard_map.100 = f32[576,128]{1,0:T(8,128)} custom-call(s32[64]{0:T(128)} %refs_0_.1, s32[64]{0:T(128)} %refs_1_.1, f32[128,128]{1,0:T(8,128)} %bitcast.12, f32[64,128]{1,0:T(8,128)} %refs_3_.1, f32[64,128]{1,0:T(8,128)} %refs_4_.1), custom_call_target="tpu_custom_call" | custom-call | flops 1000000 | bytes 500000 | tf_op jit(solution)/shard_map/pallas_call | solution.py:403
  1.9 0.0 copy-start.2
  1.9 22.1 %all-to-all-start = ((f32[64,1,1152]{2,1,0:T(1,128)}), f32[64,1,1152]{2,1,0:T(1,128)S(1)}, u32[]{:S(2)}, u32[]{:S(2)}) async-start(f32[64,1,1152]{2,1,0:T(1,128)} %bitcast.11), calls=%async_computation | async-start | bytes 589824 | tf_op jit(solution)/shard_map/all_to_all | solution.py:352
  24.0 0.0 copy-start.3
  24.0 12.8 %all-to-all-done = f32[64,1,1152]{2,1,0:T(1,128)S(1)} async-done(((f32[64,1,1152]{2,1,0:T(1,128)}), f32[64,1,1152]{2,1,0:T(1,128)S(1)}, u32[]{:S(2)}, u32[]{:S(2)}) %all-to-all-start) | async-done | bytes 294944 | tf_op jit(solution)/shard_map/all_to_all | solution.py:352
  36.9 0.0 copy-done.2
  36.9 0.0 copy-done.3
  36.9 0.0 copy-start.4
  36.9 0.0 copy-start.1
  36.9 5.9 %shard_map.101 = f32[512,128]{1,0:T(8,128)} custom-call(f32[576,128]{1,0:T(8,128)S(1)} %bitcast.7, f32[64,128]{1,0:T(8,128)S(1)} %copy-done.3, bf16[128,256]{1,0:T(8,128)(2,1)S(1)} %copy-done.2), custom_call_target="tpu_custom_call" | custom-call | flops 1000000000 | bytes 1000000 | tf_op jit(solution)/shard_map/pallas_call | solution.py:424
  42.8 0.0 copy-start
  42.8 10.7 %all-to-all-start.1 = ((f32[32,16,128]{2,1,0:T(8,128)}), f32[32,16,128]{2,1,0:T(8,128)S(1)}, u32[]{:S(2)}, u32[]{:S(2)}) async-start(f32[32,16,128]{2,1,0:T(8,128)} %bitcast.3), calls=%async_computation.1 | async-start | bytes 524288 | tf_op jit(solution)/shard_map/all_to_all | solution.py:352
  53.5 0.0 copy-done.4
  53.5 1.1 %fusion.4 = (f32[512,128]{1,0:T(8,128)S(1)}, f32[512,128]{1,0:T(8,128)S(1)}) fusion(f32[128]{0:T(128)S(1)} %get-tuple-element.7, f32[512]{0:T(512)S(1)} %copy-done.4, f32[128]{0:T(128)S(1)} %get-tuple-element.8), kind=kLoop, calls=%fused_computation.6 | loop fusion | flops 393216 | bytes 527360 | tf_op jit(solution)/shard_map/sin | solution.py:395
  54.6 2.9 %all-to-all-done.1 = f32[32,16,128]{2,1,0:T(8,128)S(1)} async-done(((f32[32,16,128]{2,1,0:T(8,128)}), f32[32,16,128]{2,1,0:T(8,128)S(1)}, u32[]{:S(2)}, u32[]{:S(2)}) %all-to-all-start.1) | async-done | bytes 262176 | tf_op jit(solution)/shard_map/all_to_all | solution.py:352
  57.5 0.0 copy-done.1
  57.5 0.0 copy-done
  57.5 1.2 %shard_map.102 = f32[128,128]{1,0:T(8,128)S(1)} custom-call(f32[512,128]{1,0:T(8,128)S(1)} %bitcast.8, bf16[1024,512]{1,0:T(8,128)(2,1)S(1)} %copy-done.1, bf16[1024,512]{1,0:T(8,128)(2,1)S(1)} %copy-done, f32[512,128]{1,0:T(8,128)S(1)} %get-tuple-element.6.cos_ref, f32[512,128]{1,0:T(8,128)S(1)} %get-tuple-element.5.sin_ref), custom_call_target="tpu_custom_call" | custom-call | flops 1000000000 | bytes 3000000 | tf_op jit(solution)/shard_map/pallas_call | solution.py:444
  58.7 17.5 %all_to_all.15 = f32[64,2,128]{2,1,0:T(2,128)S(1)} all-to-all(f32[64,2,128]{2,1,0:T(2,128)S(1)} %bitcast.10), channel_id=1, replica_groups={{320,328,336,344,352,360,368,376,256,264,272,280,288,296,304,312,448,45..., dimensions={0} | all-to-all | bytes 131072 | tf_op jit(solution)/shard_map/all_to_all | solution.py:352
  76.3 0.7 shard_map.103
  (1 shorter events, 0.0 us)
Async XLA Ops:
  1.9 35.0 %copy-start.2 = (bf16[128,256]{1,0:T(8,128)(2,1)S(1)}, bf16[128,256]{1,0:T(8,128)(2,1)}, u32[]{:S(2)}) copy-start(bf16[128,256]{1,0:T(8,128)(2,1)} %constant.86.clone.last_ref) | copy-start | bytes 196612
  1.9 34.9 %all-to-all-start = ((f32[64,1,1152]{2,1,0:T(1,128)}), f32[64,1,1152]{2,1,0:T(1,128)S(1)}, u32[]{:S(2)}, u32[]{:S(2)}) async-start(f32[64,1,1152]{2,1,0:T(1,128)} %bitcast.11), calls=%async_computation | async-start | bytes 589824 | tf_op jit(solution)/shard_map/all_to_all | solution.py:352
  24.0 12.9 %copy-start.3 = (f32[64,128]{1,0:T(8,128)S(1)}, f32[64,128]{1,0:T(8,128)}, u32[]{:S(2)}) copy-start(f32[64,128]{1,0:T(8,128)} %constant.85.clone.twist_ref) | copy-start | bytes 98308
  36.9 16.6 %copy-start.4 = (f32[512]{0:T(512)S(1)}, f32[512]{0:T(512)}, u32[]{:S(2)}) copy-start(f32[512]{0:T(512)} %constant.96) | copy-start | bytes 6148
  36.9 20.7 %copy-start.1 = (bf16[1024,512]{1,0:T(8,128)(2,1)S(1)}, bf16[1024,512]{1,0:T(8,128)(2,1)}, u32[]{:S(2)}) copy-start(bf16[1024,512]{1,0:T(8,128)(2,1)} %constant.87.clone.upper_ref) | copy-start | bytes 3145732
  42.8 14.8 %copy-start = (bf16[1024,512]{1,0:T(8,128)(2,1)S(1)}, bf16[1024,512]{1,0:T(8,128)(2,1)}, u32[]{:S(2)}) copy-start(bf16[1024,512]{1,0:T(8,128)(2,1)} %constant.88.clone.lower_ref) | copy-start | bytes 3145732
  42.8 14.7 %all-to-all-start.1 = ((f32[32,16,128]{2,1,0:T(8,128)}), f32[32,16,128]{2,1,0:T(8,128)S(1)}, u32[]{:S(2)}, u32[]{:S(2)}) async-start(f32[32,16,128]{2,1,0:T(8,128)} %bitcast.3), calls=%async_computation.1 | async-start | bytes 524288 | tf_op jit(solution)/shard_map/all_to_all | solution.py:352
